TPU v7x, 32 devices: a whole 2x2x4 slice. The times are simulated.
32 devices in a mesh: prow: 8 (over z, y), pcol: 4 (over x, core).
Axes of the slice: x: 2, y: 2, z: 4, core: 2. Of those that a mesh axis runs over, the one named last changes fastest.
Arguments:
- ainv: float32 [20480, 20480], P('prow', 'pcol'), may hold values from -0.15625 to 0.15625
- panels: float32 [3, 20480, 512], P(None, ('prow', 'pcol')), may hold values from -0.8 to 0.8
- ancestors: int32 [3, 2560], P(None, ('prow', 'pcol')), may hold values from 0 to 1, as said below
- dinv: float32 [3, 512, 512], P(None, 'prow', 'pcol'), may hold values from -6 to 6
Outputs:
- u_panel: float32 [3, 20480, 512], P(None, ('prow', 'pcol'))
- diag: float32 [3, 512, 512], P(None, 'prow', 'pcol')
Inputs may be any that keep to these rules, and one draw needn't show every extreme that they name: `ancestors`: each entry is 0 or 1; the share of ancestor blocks varies strongly between regions of the rows.
All inputs are finite; a program needn't handle non-finite values.
Results may differ from a plain program's by a relative error of at most 0.00007.
Values sent between devices are 32-bit elements; how exact they have to be, the bound alone decides.
No kernel may reach another device: no remote copies, remote signals or barrier semaphores. Data moves between devices by JAX's collectives and lax.ppermute only.
A program may use at most 192 MiB of HBM per device.

v0:
```python
import jax
import jax.numpy as jnp
from jax import lax
from jax.sharding import PartitionSpec as P

NSUP = 3
BLK = 8


def apply_rows(columns, piece):
    return jnp.dot(columns, piece, precision=lax.Precision.HIGHEST)


def on_device(ainv, panels, ancestors, dinv):
    row_flags = jnp.repeat(ancestors, BLK, axis=1).astype(jnp.float32)
    masked = panels * row_flags[:, :, None]
    results = []
    for member in range(NSUP):
        summed_one = apply_rows(ainv, lax.all_gather(masked[member], "prow", axis=0, tiled=True))
        results.append(lax.psum_scatter(summed_one, "pcol", scatter_dimension=0, tiled=True))
    partial_value = jnp.stack(results, axis=0)
    u_panel = -(row_flags[:, :, None] * partial_value)
    local_terms = jnp.einsum("srn,srm->snm", masked, u_panel, precision=lax.Precision.HIGHEST)
    totals = lax.psum(local_terms, ("prow", "pcol"))
    row_count = dinv.shape[1]
    col_count = dinv.shape[2]
    row_start = lax.axis_index("prow") * row_count
    col_start = lax.axis_index("pcol") * col_count
    own_rows = lax.dynamic_slice_in_dim(totals, row_start, row_count, 1)
    own_block = lax.dynamic_slice_in_dim(own_rows, col_start, col_count, 2)
    diag = dinv - own_block
    return (u_panel, diag)


def solution(mesh):
    in_specs = (
        P("prow", "pcol"),
        P(None, ("prow", "pcol"), None),
        P(None, ("prow", "pcol")),
        P(None, "prow", "pcol"),
    )
    out_specs = (P(None, ("prow", "pcol"), None), P(None, "prow", "pcol"))
    return jax.shard_map(
        on_device, mesh=mesh, in_specs=in_specs, out_specs=out_specs, check_vma=False
    )
```

profile of v0, /device:TPU:0, one launch (start us, length us, event | category | flops | bytes accessed | tf_op | source)
XLA Modules:
  0.0 795.0 jit_solution(11285456078699479321)
XLA Ops:
  7.2 0.0 all-gather.7.cloned.1.call-start
  7.2 0.7 convert_element_type.11
  7.9 0.1 broadcast_in_dim.2
  8.0 0.1 convert_element_type.12
  8.1 5.5 copy.9
  13.6 2.4 broadcast_multiply_fusion
  16.0 2.1 fusion.16
  18.1 1.0 copy-done
  19.1 0.0 all-gather.7.cloned.1.call-update
  19.1 0.0 all-gather.9.cloned.1.call-start
  19.2 0.7 all-gather.9.cloned.1.call-update
  19.9 0.0 all-gather.11.cloned.1.call-start
  19.9 0.7 all-gather.11.cloned.1.call-update
  20.6 0.0 reduce-scatter.4.cloned.1.call-start
  20.6 152.0 %all-gather.7.cloned.1.call-done = f32[1,5120,512]{1,2,0:T(8,128)} async-done(((f32[1,640,512]{1,2,0:T(8,128)}), f32[1,5120,512]{1,2,0:T(8,128)}) %all-gather.7.cloned.1.call-update) | async-done | bytes 10485776 | tf_op jit(solution)/shard_map/all_gather | solution.py:19
  172.6 90.3 %fusion.6 = f32[2560,512]{0,1:T(8,128)} fusion(f32[2560,5120]{1,0:T(8,128)} %param.4, f32[1,5120,512]{1,2,0:T(8,128)} %all-gather.7.cloned.1.call-done), kind=kOutput, calls=%fused_computation.6 | convolution fusion | flops 80530636800 | bytes 68157440 | tf_op jit(solution)/shard_map/dot_general | solution.py:11
  262.9 0.2 reduce-scatter.6.cloned.1.call-start
  263.2 60.5 %all-gather.9.cloned.1.call-done = f32[1,5120,512]{1,2,0:T(8,128)} async-done(((f32[1,640,512]{1,2,0:T(8,128)}), f32[1,5120,512]{1,2,0:T(8,128)}) %all-gather.9.cloned.1.call-update) | async-done | bytes 10485776 | tf_op jit(solution)/shard_map/all_gather | solution.py:19
  323.7 90.3 %fusion.9 = f32[2560,512]{0,1:T(8,128)} fusion(f32[2560,5120]{1,0:T(8,128)} %param.4, f32[1,5120,512]{1,2,0:T(8,128)} %all-gather.9.cloned.1.call-done), kind=kOutput, calls=%fused_computation.7 | convolution fusion | flops 80530636800 | bytes 68157440 | tf_op jit(solution)/shard_map/dot_general | solution.py:11
  414.0 0.3 reduce-scatter.8.cloned.1.call-start
  414.3 60.5 %all-gather.11.cloned.1.call-done = f32[1,5120,512]{1,2,0:T(8,128)} async-done(((f32[1,640,512]{1,2,0:T(8,128)}), f32[1,5120,512]{1,2,0:T(8,128)}) %all-gather.11.cloned.1.call-update) | async-done | bytes 10485776 | tf_op jit(solution)/shard_map/all_gather | solution.py:19
  474.8 90.4 %fusion.12 = f32[2560,512]{0,1:T(8,128)} fusion(f32[2560,5120]{1,0:T(8,128)} %param.4, f32[1,5120,512]{1,2,0:T(8,128)} %all-gather.11.cloned.1.call-done), kind=kOutput, calls=%fused_computation.8 | convolution fusion | flops 80530636800 | bytes 68157440 | tf_op jit(solution)/shard_map/dot_general | solution.py:11
  565.2 0.3 all-reduce.2.cloned.1.call-start
  565.5 0.0 reduce-scatter.4.cloned.1.call-done
  565.5 15.2 %reduce-scatter.6.cloned.1.call-done = f32[640,512]{0,1:T(8,128)} async-done(((f32[2560,512]{0,1:T(8,128)}), f32[640,512]{0,1:T(8,128)}) %reduce-scatter.6.cloned.1.call-update) | async-done | bytes 1310736 | tf_op jit(solution)/shard_map/reduce_scatter | solution.py:20
  580.8 53.8 %reduce-scatter.8.cloned.1.call-done = f32[640,512]{0,1:T(8,128)} async-done(((f32[2560,512]{0,1:T(8,128)}), f32[640,512]{0,1:T(8,128)}) %reduce-scatter.8.cloned.1.call-update) | async-done | bytes 1310736 | tf_op jit(solution)/shard_map/reduce_scatter | solution.py:20
  634.5 2.5 fusion.15
  637.1 1.8 copy-done.2
  638.9 9.4 %fusion.17 = f32[3,512,512]{2,1,0:T(8,128)} fusion(f32[3,640,512]{1,2,0:T(8,128)S(1)} %copy-done.1, f32[3,640,512]{1,2,0:T(8,128)S(1)} %fusion.15), kind=kOutput, calls=%fused_computation.14 | convolution fusion | flops 6039797760 | bytes 11010048 | tf_op jit(solution)/shard_map/srn,srm->snm/dot_general | solution.py:23
  648.3 5.5 copy.11
  653.8 132.3 %all-reduce.2.cloned.1.call-done = f32[3,512,512]{2,1,0:T(8,128)} async-done(((f32[3,512,512]{2,1,0:T(8,128)}), f32[3,512,512]{2,1,0:T(8,128)}) %all-reduce.2.cloned.1.call-update) | async-done | bytes 3145744 | tf_op jit(solution)/shard_map/psum | solution.py:24
  786.1 1.7 dynamic-slice_subtract_fusion
  (10 shorter events, 0.1 us)
Async XLA Ops:
  7.2 165.4 %all-gather.7.cloned.1.call-start = ((), (), s32[]{:S(2)}) async-start(), calls=%async_computation.7 | async-start | bytes 11796480 | tf_op jit(solution)/shard_map/all_gather | solution.py:19
  15.9 3.1 copy-start
  19.1 304.6 %all-gather.9.cloned.1.call-start = ((), (), s32[]{:S(2)}) async-start(), calls=%async_computation.8 | async-start | bytes 11796480 | tf_op jit(solution)/shard_map/all_gather | solution.py:19
  19.9 454.9 %all-gather.11.cloned.1.call-start = ((), (), s32[]{:S(2)}) async-start(), calls=%async_computation.9 | async-start | bytes 11796480 | tf_op jit(solution)/shard_map/all_gather | solution.py:19
  20.6 544.9 %reduce-scatter.4.cloned.1.call-start = ((), (), s32[]{:S(2)}) async-start(), calls=%async_computation.3 | async-start | bytes 6553600 | tf_op jit(solution)/shard_map/reduce_scatter | solution.py:20
  262.9 317.8 %reduce-scatter.6.cloned.1.call-start = ((), (), s32[]{:S(2)}) async-start(), calls=%async_computation.4 | async-start | bytes 6553600 | tf_op jit(solution)/shard_map/reduce_scatter | solution.py:20
  414.0 220.5 %reduce-scatter.8.cloned.1.call-start = ((), (), s32[]{:S(2)}) async-start(), calls=%async_computation.5 | async-start | bytes 6553600 | tf_op jit(solution)/shard_map/reduce_scatter | solution.py:20
  565.2 220.9 %all-reduce.2.cloned.1.call-start = ((), (), s32[]{:S(2)}) async-start(), calls=%async_computation.6 | async-start | bytes 6291456 | tf_op jit(solution)/shard_map/psum | solution.py:24
  634.5 4.4 copy-start.1
  637.1 1.9 copy-start.2
  648.3 137.8 %copy-start.3 = (f32[3,64,128]{2,1,0:T(8,128)S(1)}, f32[3,64,128]{2,1,0:T(8,128)}, u32[]{:S(2)}) copy-start(f32[3,64,128]{2,1,0:T(8,128)} %param.7) | copy-start | bytes 294916
Sparse Core Ops, SparseCore 0:
  19.2 153.3 all-gather.6
  174.8 148.8 all-gather.8
  325.9 148.8 all-gather.10
  477.2 49.5 reduce-scatter.3
  529.4 51.3 reduce-scatter.5
  583.1 51.3 reduce-scatter.7
  648.4 137.5 all-reduce.1
where the time goes:
time: 804 us; the launch traced here: 795 us
  waiting for transfers between devices  476 us (59%)
  matrix products  280 us (35%)
  local copies, waits for them, and re-layouts  16.1 us (2%)
  between operations  14.6 us (2%)
    all_gather x3, waiting for transfers between devices, on_device(): lax.all_gather(masked[member], 'prow', axis=0, tiled=True)  273 us
    dot_general x3, matrix products, apply_rows(): return jnp.dot(columns, piece, precision=lax.Precision.HIGHEST)  271 us
    psum x1, waiting for transfers between devices, on_device(): totals = lax.psum(local_terms, ('prow', 'pcol'))  132 us
    reduce_scatter x3, waiting for transfers between devices, on_device(): lax.psum_scatter(summed_one, 'pcol', scatter_dimension=0, tiled=True)  69 us
  transfers between devices with their start and end apart: 7, of which 6 were waited for; matrix products, arithmetic and copies ran while one was open for 35% of the time, Pallas kernels for 0%

commit v1 on v0

v1 whole, which is shorter than its diff:
```python
import functools

import jax
import jax.numpy as jnp
from jax import lax
from jax.experimental import pallas as pl
from jax.experimental.pallas import tpu as pltpu
from jax.sharding import PartitionSpec as P

LANES = 128
CHAIN = 4


def is_power_of_two(n):
    return n > 0 and n & (n - 1) == 0


def plain_on_device(ainv, panels, ancestors, dinv):
    block = panels.shape[1] // ancestors.shape[1]
    row_flags = jnp.repeat(ancestors, block, axis=1).astype(jnp.float32)
    masked = panels * row_flags[:, :, None]
    results = []
    for member in range(panels.shape[0]):
        gathered = lax.all_gather(masked[member], "prow", axis=0, tiled=True)
        summed_one = jnp.dot(ainv, gathered, precision=lax.Precision.HIGHEST)
        results.append(lax.psum_scatter(summed_one, "pcol", scatter_dimension=0, tiled=True))
    u_panel = -(row_flags[:, :, None] * jnp.stack(results, axis=0))
    local_terms = jnp.einsum("srn,srm->snm", masked, u_panel, precision=lax.Precision.HIGHEST)
    totals = lax.psum(local_terms, ("prow", "pcol"))
    row_count, col_count = dinv.shape[1:]
    own_rows = lax.dynamic_slice_in_dim(totals, lax.axis_index("prow") * row_count, row_count, 1)
    own_block = lax.dynamic_slice_in_dim(own_rows, lax.axis_index("pcol") * col_count, col_count, 2)
    return u_panel, dinv - own_block


def follow(value, earlier):
    earlier = [array for array in earlier if array is not None]
    return lax.optimization_barrier((value, *earlier))[0] if earlier else value


def split(x):
    high = x.astype(jnp.bfloat16)
    low = (x - high.astype(jnp.float32)).astype(jnp.bfloat16)
    return high, low


def product_kernel(piece_counts, has_sum, n_out, *refs):
    n_items = len(piece_counts)
    refs = refs[1:]
    a_refs, refs = refs[:n_items], refs[n_items:]
    n_pieces = sum(piece_counts)
    piece_refs, refs = refs[:n_pieces], refs[n_pieces:]
    if has_sum:
        sum_ref, refs = refs[0], refs[1:]
    out_refs, (token_ref, high_ref, low_ref) = refs[:n_out], refs[n_out:]

    @pl.when(pl.program_id(0) == 0)
    def _():
        row = 0
        for piece in piece_refs:
            rows = piece.shape[0]
            high_ref[row : row + rows, :], low_ref[row : row + rows, :] = split(piece[...])
            row += rows
        token_ref[...] = jnp.zeros_like(token_ref)

    halves = [split(a_ref[...]) for a_ref in a_refs]
    a_high = jnp.concatenate([high for high, _ in halves], axis=1)
    a_low = jnp.concatenate([low for _, low in halves], axis=1)
    times = functools.partial(jnp.dot, preferred_element_type=jnp.float32)
    total = times(a_high, high_ref[...]) + (times(a_low, high_ref[...]) + times(a_high, low_ref[...]))
    if has_sum:
        total = sum_ref[...] + total
    if n_out == 1:
        out_refs[0][...] = total
    else:
        away = pl.program_id(0) < pl.num_programs(0) // 2

        @pl.when(away)
        def _():
            out_refs[1][...] = total

        @pl.when(jnp.logical_not(away))
        def _():
            out_refs[0][...] = total


def add_products(ainv, column, items, regions, running, tile, parted=False, after=()):
    depth = sum(piece.shape[0] for piece in items[0])
    width = items[0][0].shape[1]
    blocks = ainv.shape[0] // depth
    per = depth // tile
    steps = blocks * per
    n_items = len(items)
    prefetch = follow(jnp.stack([column, *regions]).astype(jnp.int32), after)

    def row_of(i):
        if not parted:
            return i
        away = i < steps // 2
        j = jnp.where(away, i, i - steps // 2)
        return (2 * (j // per) + jnp.where(away, 1, 0)) * per + j % per

    def a_row(i, s):
        row = row_of(i)
        return ((row // per) ^ s[0]) * per + row % per

    once = pl.Buffered(buffer_count=1)
    in_specs = [
        pl.BlockSpec((tile, depth), functools.partial(lambda k, i, s: (a_row(i, s), s[k]), k + 1))
        for k in range(n_items)
    ]
    pieces = [piece for item in items for piece in item]
    in_specs += [pl.BlockSpec(piece.shape, lambda i, s: (0, 0), pipeline_mode=once) for piece in pieces]
    operands = [ainv] * n_items + pieces
    aliases = {}
    if running is not None:
        if not parted:
            aliases = {len(operands) + 1: 0}
        in_specs.append(pl.BlockSpec((tile, width), lambda i, s: (row_of(i), 0)))
        operands.append(running)
    rows = blocks * depth
    if parted:
        out_shape = [jax.ShapeDtypeStruct((rows // 2, width), jnp.float32)] * 2
        out_specs = [
            pl.BlockSpec((tile, width), lambda i, s: (jnp.maximum(i - steps // 2, 0), 0)),
            pl.BlockSpec((tile, width), lambda i, s: (jnp.minimum(i, steps // 2 - 1), 0)),
        ]
    else:
        out_shape = [jax.ShapeDtypeStruct((rows, width), jnp.float32)]
        out_specs = [pl.BlockSpec((tile, width), lambda i, s: (i, 0))]
    n_out = len(out_shape)
    out_shape.append(jax.ShapeDtypeStruct((8, LANES), jnp.float32))
    out_specs.append(pl.BlockSpec((8, LANES), lambda i, s: (0, 0)))
    outs = pl.pallas_call(
        functools.partial(product_kernel, tuple(len(item) for item in items), running is not None, n_out),
        out_shape=out_shape,
        grid_spec=pltpu.PrefetchScalarGridSpec(
            num_scalar_prefetch=1,
            grid=(steps,),
            in_specs=in_specs,
            out_specs=out_specs,
            scratch_shapes=[pltpu.VMEM((n_items * depth, width), jnp.bfloat16)] * 2,
        ),
        input_output_aliases=aliases,
        cost_estimate=pl.CostEstimate(flops=1, bytes_accessed=1, transcendentals=0),
        compiler_params=pltpu.CompilerParams(vmem_limit_bytes=52 * 1024 * 1024),
    )(prefetch, *operands)
    return tuple(outs)


def chain_order(length):
    orders = [[place] for place in range(length)]
    span = 1
    while span < length:
        grown = []
        for place in range(length):
            block = place // span
            edge = (block + 1) * span if block % 2 == 0 else block * span - 1
            grown.append(orders[place] + orders[edge][:span])
        orders = grown
        span *= 2
    return orders


def chain_hops(length, span):
    hops = [[] for _ in range(span)]
    for start in range(0, length, 2 * span):
        for hop in range(span):
            below, above = start + span - 1 - hop, start + span + hop
            if hop == 0:
                hops[0] += [(below, above), (above, below)]
            else:
                hops[hop] += [(below + 1, below), (above - 1, above)]
    return hops


def column_groups(sups, wide):
    last = wide // 2
    each = (sups * wide - last) // 2
    groups, at = [], 0
    for size in (each, each, last):
        pieces, end = [], at + size
        while at < end:
            member, start = at // wide, at % wide
            width = min(wide - start, end - at)
            pieces.append((member, start, width))
            at += width
        groups.append(pieces)
    return groups


def fast_on_device(n_prow, n_pcol, ainv, panels, ancestors, dinv):
    sups, depth, wide = panels.shape
    length = n_prow // 2
    half = depth // 2
    own_p = lax.axis_index("prow")
    own_c = lax.axis_index("pcol")
    place, side = own_p // 2, own_p % 2
    flags = jnp.repeat(ancestors, depth // ancestors.shape[1], axis=1).astype(jnp.float32)
    cols, rows_own = dinv.shape[2], dinv.shape[1]

    side_pairs = [(p, p ^ 1) for p in range(n_prow)]

    def chain_pairs(pairs):
        return [(2 * a + y, 2 * b + y) for a, b in pairs for y in (0, 1)]

    def prow_pairs(bit):
        return [(p, p ^ bit) for p in range(n_prow)]

    def pcol_pairs(bit):
        return [(c, c ^ bit) for c in range(n_pcol)]

    prow_bits = [1 << k for k in range(n_prow.bit_length() - 1)]
    pcol_bits = [1 << k for k in range(n_pcol.bit_length() - 1)]

    orders = chain_order(length)
    own_order = [jnp.take(jnp.array(column, jnp.int32), place) for column in zip(*orders)]
    same_side = [2 * z + side for z in own_order]
    other_side = [2 * z + 1 - side for z in own_order]

    masked = [panels[member] * flags[member][:, None] for member in range(sups)]
    due = {}

    def want(tick, *arrays):
        due.setdefault(tick, []).extend(arrays)

    class Group:
        def __init__(self, pieces):
            self.pieces = pieces
            self.here = [jnp.concatenate([masked[m][:, at : at + width] for m, at, width in pieces], axis=1)]
            self.there = []
            self.running = None

    first_group, second_group, last_group = [Group(pieces) for pieces in column_groups(sups, wide)]

    def moves(group, step, after):
        hops1 = chain_pairs(chain_hops(length, 1)[0])
        send = lambda value, pairs: lax.ppermute(follow(value, after), "prow", pairs)
        here, there = group.here, group.there
        new = []
        if step == 0:
            there.append([send(here[0], side_pairs)])
            new.append(there[0][0])
            group.first = send(here[0], hops1)
            new.append(group.first)
            if length >= 4:
                hops2 = chain_hops(length, 2)
                group.over = send(here[0], chain_pairs(hops2[0]))
                new.append(group.over)
            here.append(group.first)
        elif step == 1:
            there.append([send(here[1][:half], side_pairs)])
            new.append(there[1][0])
            if length >= 4:
                hops2 = chain_hops(length, 2)
                inward = send(group.over, chain_pairs(hops2[1]))
                group.over2 = send(here[1], chain_pairs(hops2[0]))
                new += [inward, group.over2]
                here.append(jnp.where(at_edge, group.over, inward))
        elif step == 2:
            inward = send(group.over2, chain_pairs(chain_hops(length, 2)[1]))
            there.append([send(here[2], side_pairs)])
            new += [inward, there[2][0]]
            here.append(jnp.where(at_edge, group.over2, inward))
        elif step == 3:
            second = send(there[0][0][half:], hops1)
            there[1].append(second)
            there.append([send(here[3], side_pairs)])
            new += [second, there[3][0]]
        return new

    at_edge = jnp.logical_or(place == length // 2 - 1, place == length // 2)

    def items(group, step):
        here, there = group.here, group.there
        wanted = [((0, 0), (1, 0)), ((0, 1), (0, 2)), ((0, 3), (1, 2)), ((1, 3), (1, 1))][step]
        return [(there[k], other_side[k]) if over else ([here[k]], same_side[k]) for over, k in wanted]

    def sum_rows(kept, away, tick):
        for index, bit in enumerate(pcol_bits):
            if tick + 1 + index < len(arrived):
                away = follow(away, arrived[tick + 1 + index])
            received = lax.ppermute(away, "pcol", pcol_pairs(bit))
            total = kept + received
            if total.shape[0] == depth:
                want(tick + 5, received)
                return total
            blocks = total.reshape(total.shape[0] // (2 * depth), 2, depth, total.shape[1])
            kept = blocks[:, 0].reshape(-1, total.shape[1])
            away = blocks[:, 1].reshape(-1, total.shape[1])
            want(tick + 2 if tick + 2 < len(ticks) else tick + 1, away)

    def sum_diagonal(terms, start, tick):
        width = terms.shape[2]
        count = width // cols
        low_bits = [bit for bit in pcol_bits if bit < count]
        blocks = {
            q: lax.dynamic_slice_in_dim(terms, ((own_c ^ q) % count) * cols, cols, 2) for q in range(count)
        }
        for bit in low_bits:
            away = [q for q in sorted(blocks) if q & bit]
            moved = lax.ppermute(jnp.stack([blocks[q] for q in away]), "pcol", pcol_pairs(bit))
            want(tick, moved)
            tick += 1
            blocks = {q ^ bit: blocks[q ^ bit] + moved[k] for k, q in enumerate(away)}
        value = blocks[0].reshape(terms.shape[0], n_prow, rows_own, cols)
        for bit in prow_bits:
            paired = value.reshape(value.shape[0], value.shape[1] // 2, 2, rows_own, cols)
            mine = (own_p // bit) % 2
            keep = lax.dynamic_index_in_dim(paired, mine, 2, keepdims=False)
            send = lax.dynamic_index_in_dim(paired, 1 - mine, 2, keepdims=False)
            value = keep + lax.ppermute(send, "prow", prow_pairs(bit))
            want(tick, value)
            tick += 1
        value = value[:, 0]
        for bit in pcol_bits:
            if bit not in low_bits:
                value = value + lax.ppermute(value, "pcol", pcol_pairs(bit))
        return value

    def transposed_product(left, right):
        return lax.dot_general(
            left, right, (((0,), (0,)), ((), ())), precision=lax.Precision.HIGH,
            preferred_element_type=jnp.float32,
        )

    near = [masked[-1]]
    for index, bit in enumerate(pcol_bits):
        moved = [lax.ppermute(value, "pcol", pcol_pairs(bit)) for value in near]
        want(1 + 2 * index, *moved)
        near += moved
    near_kept = jnp.concatenate(near[0::2], axis=0)
    near_away = jnp.concatenate(near[1::2], axis=0)

    ticks = [(group, step) for step in range(4) for group in (first_group, second_group)]
    ticks += [(last_group, step) for step in range(4)]
    turns = 8
    arrived, tokens = [], []
    parts = [[] for _ in range(sups)]
    diag = [[] for _ in range(sups)]

    def start(k):
        group, step = ticks[k]
        lead = 2 if k <= turns else 1
        after = (arrived[k - lead] if k >= lead else []) + ([tokens[k - lead - 1]] if k > lead else [])
        arrived.append(moves(group, step, after))

    started = 0
    for k, (group, step) in enumerate(ticks):
        while started < len(ticks) and started <= (k + 2 if k + 2 <= turns else max(k + 1, turns)):
            start(started)
            started += 1
        if k == len(ticks) - 1:
            products = [
                transposed_product(masked[m], follow(jnp.concatenate(parts[m], axis=1), tokens[-1:]))
                for m in range(sups - 1)
            ]
            for m, value in enumerate(sum_diagonal(jnp.stack(products), 0, k + 1)):
                diag[m].append(value)
        chosen = items(group, step)
        last = step == 3
        *sums, token = add_products(
            ainv, own_c, [c[0] for c in chosen], [c[1] for c in chosen], group.running, depth,
            parted=last, after=arrived[k] + (tokens[-1:]) + due.get(k, []),
        )
        tokens.append(token)
        if not last:
            group.running = sums[0]
            continue
        kept, away = sums
        if group is last_group:
            diag[-1].append(-(transposed_product(near_kept, kept) + transposed_product(near_away, away)))
        summed = sum_rows(kept, away, k)
        at = 0
        for member, _, width in group.pieces:
            part = -(flags[member][:, None] * summed[:, at : at + width])
            at += width
            parts[member].append(part)
            if member == sups - 1 and group is not last_group:
                diag[-1].append(transposed_product(masked[member], follow(part, tokens[-1:])))
    u_panel = jnp.stack([jnp.concatenate(part, axis=1) for part in parts])
    diag[-1] = [sum_diagonal(jnp.concatenate(diag[-1], axis=1)[None], 0, len(ticks))[0]]
    return u_panel, dinv - jnp.stack([found[0] for found in diag])


def solution(mesh):
    n_prow, n_pcol = mesh.shape["prow"], mesh.shape["pcol"]

    def on_device(ainv, panels, ancestors, dinv):
        depth, wide = panels.shape[1:]
        fits = (
            is_power_of_two(n_prow)
            and is_power_of_two(n_pcol)
            and n_prow == 2 * CHAIN
            and (2 * panels.shape[0] - 1) * wide % (4 * LANES) == 0
            and panels.shape[0] >= 2
            and n_pcol >= 2
            and depth % LANES == 0
            and wide % (2 * LANES) == 0
            and wide % n_prow == 0
            and ainv.shape == (depth * n_pcol, depth * n_prow)
        )
        if fits:
            return fast_on_device(n_prow, n_pcol, ainv, panels, ancestors, dinv)
        return plain_on_device(ainv, panels, ancestors, dinv)

    in_specs = (
        P("prow", "pcol"),
        P(None, ("prow", "pcol"), None),
        P(None, ("prow", "pcol")),
        P(None, "prow", "pcol"),
    )
    out_specs = (P(None, ("prow", "pcol"), None), P(None, "prow", "pcol"))
    return jax.shard_map(on_device, mesh=mesh, in_specs=in_specs, out_specs=out_specs, check_vma=False)
```

time: 804 us -> 487 us (0.61)
  waiting for transfers between devices: 476 us -> 126 us
  matrix products: 280 us -> 11.2 us
  Pallas kernels: 0 us -> 227 us
  starting transfers between devices: 0.92 us -> 64.3 us
  other arithmetic: 7.25 us -> 25.5 us
  between operations: 14.6 us -> 3.78 us
    all_gather x3 -> x0, waiting for transfers between devices: 273 us -> none  [on_device(): lax.all_gather(masked[member], 'prow', axis=0, tiled=True)]
    dot_general x4 -> x5, matrix products: 280 us -> 11.2 us  [transposed_product(): lax.dot_general(left, right, (((0,), (0,)), ((), ())), precision=lax.Prec...]
    pallas_call x0 -> x12, Pallas kernels: none -> 227 us  [add_products(): pl.pallas_call(functools.partial(product_kernel, tuple((len(item) for ite...]
    psum x1 -> x0, waiting for transfers between devices: 132 us -> none  [on_device(): totals = lax.psum(local_terms, ('prow', 'pcol'))]
    ppermute x0 -> x49, waiting for transfers between devices: none -> 126 us  [the longest x30 87.2 us: moves(): lax.ppermute(follow(value, after), 'prow', pairs)]
    reduce_scatter x3 -> x0, waiting for transfers between devices: 69 us -> none  [on_device(): lax.psum_scatter(summed_one, 'pcol', scatter_dimension=0, tiled=True)]
    ppermute x0 -> x49, starting transfers between devices: none -> 64.3 us  [the longest x30 43 us: moves(): lax.ppermute(follow(value, after), 'prow', pairs)]
    add x0 -> x12, other arithmetic: none -> 8.26 us  [the longest x5 7.95 us: sum_rows(): total = kept + received]
  transfers between devices with their start and end apart: 7 -> 49, of which waited for: 6 -> 18; matrix products, arithmetic and copies ran while one was open for 35% -> 10% of each run, Pallas kernels for 0% -> 47%
where the time goes in v1:
time: 487 us; the launch traced here: 479 us
  Pallas kernels  227 us (47%)
  waiting for transfers between devices  126 us (26%)
  starting transfers between devices  64.3 us (13%)
  other arithmetic  25.5 us (5%)
  local copies, waits for them, and re-layouts  21.3 us (4%)
  matrix products  11.2 us (2%)
    pallas_call x12, Pallas kernels, add_products(): pl.pallas_call(functools.partial(product_kernel, tuple((len(item) for ite...  227 us
    ppermute x30, waiting for transfers between devices, moves(): lax.ppermute(follow(value, after), 'prow', pairs)  87.2 us
    ppermute x30, starting transfers between devices, moves(): lax.ppermute(follow(value, after), 'prow', pairs)  43 us
    ppermute x6, waiting for transfers between devices, sum_rows(): received = lax.ppermute(away, 'pcol', pcol_pairs(bit))  23 us
    ppermute x6, starting transfers between devices, sum_diagonal(): value = keep + lax.ppermute(send, 'prow', prow_pairs(bit))  11.4 us
    dot_general x5, matrix products, transposed_product(): lax.dot_general(left, right, (((0,), (0,)), ((), ())), precision=lax.Prec...  11.2 us
  transfers between devices with their start and end apart: 49, of which 18 were waited for; matrix products, arithmetic and copies ran while one was open for 10% of the time, Pallas kernels for 47%

profile of v1, /device:TPU:0, one launch (start us, length us, event | category | flops | bytes accessed | tf_op | source)
XLA Modules:
  0.0 478.9 jit_solution(14411174421425783411)
XLA Ops:
  1.9 3.5 bitcast_multiply_fusion.2
  8.3 4.7 collective-permute-start.1
  20.9 28.9 %collective-permute-done.1.refs_3_ = f32[640,640]{1,0:T(8,128)} collective-permute-done((f32[640,640]{1,0:T(8,128)S(1)}, f32[640,640]{1,0:T(8,128)}, u32[]{:S(2)}, u32[]{:S(2)}) %collective-permute-start.1) | collective-permute-done | bytes 1638432 | tf_op jit(solution)/shard_map/ppermute | solution.py:238
  56.9 27.9 %collective-permute-done.7.refs_3_ = f32[640,640]{1,0:T(8,128)} collective-permute-done((f32[640,640]{1,0:T(8,128)S(1)}, f32[640,640]{1,0:T(8,128)}, u32[]{:S(2)}, u32[]{:S(2)}) %collective-permute-start.7) | collective-permute-done | bytes 1638432 | tf_op jit(solution)/shard_map/ppermute | solution.py:238
  86.5 20.7 %shard_map.95 = (f32[2560,640]{1,0:T(8,128)}, f32[8,128]{1,0:T(8,128)}) custom-call(s32[3]{0:T(128)S(1)} %pad_add_fusion.1.refs_0_, f32[2560,5120]{1,0:T(8,128)} %refs_2_.23, f32[2560,5120]{1,0:T(8,128)} %refs_2_.23, f32[640,640]{1,0:T(8,128)S(1)} %pad_maximum_fusion.1.refs_3_, f32[640,640]{1,0:T(8,128)} %copy-done.17), custom_call_target="tpu_custom_call" | custom-call | flops 1 | bytes 1 | tf_op jit(solution)/shard_map/pallas_call | solution.py:134
  113.0 7.0 %collective-permute-done.5 = f32[640,640]{1,0:T(8,128)} collective-permute-done((f32[640,640]{1,0:T(8,128)}, f32[640,640]{1,0:T(8,128)}, u32[]{:S(2)}, u32[]{:S(2)}) %collective-permute-start.5) | collective-permute-done | bytes 1638432 | tf_op jit(solution)/shard_map/ppermute | solution.py:238
  121.5 20.7 %shard_map.96 = (f32[2560,640]{1,0:T(8,128)}, f32[8,128]{1,0:T(8,128)}) custom-call(s32[3]{0:T(128)S(1)} %pad_add_fusion.1.refs_0_, f32[2560,5120]{1,0:T(8,128)} %refs_2_.23, f32[2560,5120]{1,0:T(8,128)} %refs_2_.23, f32[640,640]{1,0:T(8,128)S(1)} %pad_maximum_fusion.2.refs_3_, f32[640,640]{1,0:T(8,128)} %collective-permute-done.6.refs_4_), custom_call_target="tpu_custom_call" | custom-call | flops 1 | bytes 1 | tf_op jit(solution)/shard_map/pallas_call | solution.py:134
  149.4 5.6 %collective-permute-done.13 = f32[640,640]{1,0:T(8,128)} collective-permute-done((f32[640,640]{1,0:T(8,128)}, f32[640,640]{1,0:T(8,128)}, u32[]{:S(2)}, u32[]{:S(2)}) %collective-permute-start.13) | collective-permute-done | bytes 1638432 | tf_op jit(solution)/shard_map/ppermute | solution.py:238
  156.6 22.2 %shard_map.97 = (f32[2560,640]{1,0:T(8,128)}, f32[8,128]{1,0:T(8,128)}) custom-call(s32[3]{0:T(128)S(1)} %pad_add_fusion.2.refs_0_, f32[2560,5120]{1,0:T(8,128)} %refs_2_.23, f32[2560,5120]{1,0:T(8,128)} %refs_2_.23, f32[640,640]{1,0:T(8,128)} %collective-permute-done.1.refs_3_, f32[640,640]{1,0:T(8,128)} %copy-done.15, ...), custom_call_target="tpu_custom_call", output_to_operand_aliasing={{0}: (5, {})} | custom-call | flops 1 | bytes 1 | tf_op jit(solution)/shard_map/pallas_call | solution.py:134
  180.2 2.8 broadcast_select_fusion.2.refs_4_
  185.8 22.2 %shard_map.98 = (f32[2560,640]{1,0:T(8,128)}, f32[8,128]{1,0:T(8,128)}) custom-call(s32[3]{0:T(128)S(1)} %pad_add_fusion.2.refs_0_, f32[2560,5120]{1,0:T(8,128)} %refs_2_.23, f32[2560,5120]{1,0:T(8,128)} %refs_2_.23, f32[640,640]{1,0:T(8,128)} %collective-permute-done.7.refs_3_, ...), custom_call_target="tpu_custom_call", output_to_operand_aliasing={{0}: (5, {})} | custom-call | flops 1 | bytes 1 | tf_op jit(solution)/shard_map/pallas_call | solution.py:134
  210.2 14.0 %collective-permute-done.19 = f32[640,640]{1,0:T(8,128)} collective-permute-done((f32[640,640]{1,0:T(8,128)}, f32[640,640]{1,0:T(8,128)}, u32[]{:S(2)}, u32[]{:S(2)}) %collective-permute-start.19) | collective-permute-done | bytes 1638432 | tf_op jit(solution)/shard_map/ppermute | solution.py:238
  225.8 21.8 %shard_map.99 = (f32[2560,640]{1,0:T(8,128)}, f32[8,128]{1,0:T(8,128)}) custom-call(s32[3]{0:T(128)S(1)} %pad_add_fusion.3.refs_0_, f32[2560,5120]{1,0:T(8,128)} %refs_2_.23, f32[2560,5120]{1,0:T(8,128)} %refs_2_.23, f32[640,640]{1,0:T(8,128)S(1)} %broadcast_select_fusion.1.refs_3_, ...), custom_call_target="tpu_custom_call", output_to_operand_aliasing={{0}: (5, {})} | custom-call | flops 1 | bytes 1 | tf_op jit(solution)/shard_map/pallas_call | solution.py:134
  254.2 30.0 %shard_map.100 = (f32[2560,640]{1,0:T(8,128)}, f32[8,128]{1,0:T(8,128)}) custom-call(s32[3]{0:T(128)S(1)} %pad_add_fusion.3.refs_0_, f32[2560,5120]{1,0:T(8,128)} %refs_2_.23, f32[2560,5120]{1,0:T(8,128)} %refs_2_.23, f32[640,640]{1,0:T(8,128)S(1)} %broadcast_select_fusion.refs_3_, ...), custom_call_target="tpu_custom_call", output_to_operand_aliasing={{0}: (5, {})} | custom-call | flops 1 | bytes 1 | tf_op jit(solution)/shard_map/pallas_call | solution.py:134
  284.3 23.3 %shard_map.101 = (f32[1280,640]{1,0:T(8,128)}, f32[1280,640]{1,0:T(8,128)}, f32[8,128]{1,0:T(8,128)}) custom-call(s32[3]{0:T(128)S(1)} %pad_add_fusion.refs_0_, f32[2560,5120]{1,0:T(8,128)} %refs_2_.23, f32[2560,5120]{1,0:T(8,128)} %refs_2_.23, f32[640,640]{1,0:T(8,128)} %collective-permute-done.18.refs_3_, f32[320,640]{1,0:T(8,128)} %collective-permute-done.4.refs_4_, ...), custom_call_target="tpu_custom_call" | custom-call | flops 1 | bytes 1 | tf_op jit(solution)/shard_map/pallas_call | solution.py:134
  308.4 2.7 collective-permute-start.25
  311.6 23.2 %shard_map.102 = (f32[1280,640]{1,0:T(8,128)}, f32[1280,640]{1,0:T(8,128)}, f32[8,128]{1,0:T(8,128)}) custom-call(s32[3]{0:T(128)S(1)} %pad_add_fusion.refs_0_, f32[2560,5120]{1,0:T(8,128)} %refs_2_.23, f32[2560,5120]{1,0:T(8,128)} %refs_2_.23, f32[640,640]{1,0:T(8,128)} %collective-permute-done.22.refs_3_, f32[320,640]{1,0:T(8,128)S(1)} %copy-done.2, ...), custom_call_target="tpu_custom_call" | custom-call | flops 1 | bytes 1 | tf_op jit(solution)/shard_map/pallas_call | solution.py:134
  338.6 2.3 add.183
  344.7 10.6 %shard_map.103 = (f32[2560,256]{1,0:T(8,128)}, f32[8,128]{1,0:T(8,128)}) custom-call(s32[3]{0:T(128)S(1)} %copy-done.4, f32[2560,5120]{1,0:T(8,128)} %refs_2_.23, f32[2560,5120]{1,0:T(8,128)} %refs_2_.23, f32[640,256]{1,0:T(8,128)S(1)} %copy-done, f32[640,256]{1,0:T(8,128)S(1)} %collective-permute-done.24.refs_4_), custom_call_target="tpu_custom_call" | custom-call | flops 1 | bytes 1 | tf_op jit(solution)/shard_map/pallas_call | solution.py:134
  357.7 2.3 add.185
  362.2 10.8 %shard_map.104 = (f32[2560,256]{1,0:T(8,128)}, f32[8,128]{1,0:T(8,128)}) custom-call(s32[3]{0:T(128)S(1)} %copy-done.6, f32[2560,5120]{1,0:T(8,128)} %refs_2_.23, f32[2560,5120]{1,0:T(8,128)} %refs_2_.23, f32[640,256]{1,0:T(8,128)S(1)} %collective-permute-done.25.refs_3_, ...), custom_call_target="tpu_custom_call", output_to_operand_aliasing={{0}: (5, {})} | custom-call | flops 1 | bytes 1 | tf_op jit(solution)/shard_map/pallas_call | solution.py:134
  378.1 10.6 %shard_map.105 = (f32[2560,256]{1,0:T(8,128)}, f32[8,128]{1,0:T(8,128)}) custom-call(s32[3]{0:T(128)S(1)} %pad_add_fusion.3.refs_0_, f32[2560,5120]{1,0:T(8,128)} %refs_2_.23, f32[2560,5120]{1,0:T(8,128)} %refs_2_.23, f32[640,256]{1,0:T(8,128)S(1)} %broadcast_select_fusion.4.refs_3_, ...), custom_call_target="tpu_custom_call", output_to_operand_aliasing={{0}: (5, {})} | custom-call | flops 1 | bytes 1 | tf_op jit(solution)/shard_map/pallas_call | solution.py:134
  389.7 11.1 %shard_map.106 = (f32[1280,256]{1,0:T(8,128)}, f32[1280,256]{1,0:T(8,128)}, f32[8,128]{1,0:T(8,128)}) custom-call(s32[3]{0:T(128)S(1)} %pad_add_fusion.refs_0_, f32[2560,5120]{1,0:T(8,128)} %refs_2_.23, f32[2560,5120]{1,0:T(8,128)} %refs_2_.23, f32[640,256]{1,0:T(8,128)S(1)} %collective-permute-done.36.refs_3_, ...), custom_call_target="tpu_custom_call" | custom-call | flops 1 | bytes 1 | tf_op jit(solution)/shard_map/pallas_call | solution.py:134
  405.8 10.7 %collective-permute-done.29 = f32[640,640]{1,0:T(8,128)} collective-permute-done((f32[640,640]{1,0:T(8,128)}, f32[640,640]{1,0:T(8,128)}, u32[]{:S(2)}, u32[]{:S(2)}) %collective-permute-start.29) | collective-permute-done | bytes 1638432 | tf_op jit(solution)/shard_map/ppermute | solution.py:283
  422.6 3.0 fusion
  427.5 3.0 fusion.14
  431.4 12.3 %collective-permute-done.38 = f32[640,256]{1,0:T(8,128)S(1)} collective-permute-done((f32[640,256]{1,0:T(8,128)S(1)}, f32[640,256]{1,0:T(8,128)S(1)}, u32[]{:S(2)}, u32[]{:S(2)}) %collective-permute-start.38) | collective-permute-done | bytes 655392 | tf_op jit(solution)/shard_map/ppermute | solution.py:283
  446.4 6.8 %collective-permute-done.40 = f32[1,2,512,128]{3,2,1,0:T(8,128)S(1)} collective-permute-done((f32[1,2,512,128]{3,2,1,0:T(8,128)S(1)}, f32[1,2,512,128]{3,2,1,0:T(8,128)S(1)}, u32[]{:S(2)}, u32[]{:S(2)}) %collective-permute-start.40) | collective-permute-done | bytes 524320 | tf_op jit(solution)/shard_map/ppermute | solution.py:302
  454.0 2.3 pad_maximum_fusion
  460.2 2.4 collective-permute-start.42
  468.2 2.4 collective-permute-start.47
  475.2 2.6 collective-permute-done.48
  (219 shorter events, 100.8 us)
Async XLA Ops:
  8.3 41.5 %collective-permute-start.1 = (f32[640,640]{1,0:T(8,128)S(1)}, f32[640,640]{1,0:T(8,128)}, u32[]{:S(2)}, u32[]{:S(2)}) collective-permute-start(f32[640,640]{1,0:T(8,128)S(1)} %pad_maximum_fusion.1.refs_3_), channel_id=1, source_target_pairs={{0,8},{4,12},{8,0},{12,4},{16,24},{20,28},{24,16},{28,20},{1,9},{5... | collective-permute-start | bytes 4915208 | tf_op jit(solution)/shard_map/ppermute | solution.py:238
  13.0 38.7 %collective-permute-start = (f32[640,640]{1,0:T(8,128)S(1)}, f32[640,640]{1,0:T(8,128)S(1)}, u32[]{:S(2)}, u32[]{:S(2)}) collective-permute-start(f32[640,640]{1,0:T(8,128)S(1)} %pad_maximum_fusion.1.refs_3_), channel_id=1, source_target_pairs={{0,4},{4,0},{8,12},{12,8},{16,20},{20,16},{24,28},{28,24},{1,5},{5... | collective-permute-start | bytes 4915208 | tf_op jit(solution)/shard_map/ppermute | solution.py:238
  16.9 36.1 %collective-permute-start.8 = (f32[640,640]{1,0:T(8,128)S(1)}, f32[640,640]{1,0:T(8,128)}, u32[]{:S(2)}, u32[]{:S(2)}) collective-permute-start(f32[640,640]{1,0:T(8,128)S(1)} %pad_maximum_fusion.2.refs_3_), channel_id=1, source_target_pairs={{8,16},{12,20},{16,8},{20,12},{9,17},{13,21},{17,9},{21,13},{10,18... | collective-permute-start | bytes 4915208 | tf_op jit(solution)/shard_map/ppermute | solution.py:238
  18.8 66.1 %collective-permute-start.7 = (f32[640,640]{1,0:T(8,128)S(1)}, f32[640,640]{1,0:T(8,128)}, u32[]{:S(2)}, u32[]{:S(2)}) collective-permute-start(f32[640,640]{1,0:T(8,128)S(1)} %pad_maximum_fusion.2.refs_3_), channel_id=1, source_target_pairs={{0,8},{4,12},{8,0},{12,4},{16,24},{20,28},{24,16},{28,20},{1,9},{5... | collective-permute-start | bytes 4915208 | tf_op jit(solution)/shard_map/ppermute | solution.py:238
  20.4 86.8 %collective-permute-start.6 = (f32[640,640]{1,0:T(8,128)S(1)}, f32[640,640]{1,0:T(8,128)}, u32[]{:S(2)}, u32[]{:S(2)}) collective-permute-start(f32[640,640]{1,0:T(8,128)S(1)} %pad_maximum_fusion.2.refs_3_), channel_id=1, source_target_pairs={{0,4},{4,0},{8,12},{12,8},{16,20},{20,16},{24,28},{28,24},{1,5},{5... | collective-permute-start | bytes 4915208 | tf_op jit(solution)/shard_map/ppermute | solution.py:238
  49.7 58.7 %collective-permute-start.9 = (f32[640,512]{1,0:T(8,128)}, f32[640,512]{1,0:T(8,128)}, u32[]{:S(2)}, u32[]{:S(2)}) collective-permute-start(f32[640,512]{1,0:T(8,128)} %get-tuple-element.204), channel_id=1, source_target_pairs={{0,1},{1,0},{2,3},{3,2},{4,5},{5,4},{6,7},{7,6},{8,9},{9,8},{10,11... | collective-permute-start | bytes 3932168 | tf_op jit(solution)/shard_map/ppermute | solution.py:329
  51.7 68.2 %collective-permute-start.5 = (f32[640,640]{1,0:T(8,128)}, f32[640,640]{1,0:T(8,128)}, u32[]{:S(2)}, u32[]{:S(2)}) collective-permute-start(f32[640,640]{1,0:T(8,128)} %collective-permute-done.2), channel_id=1, source_target_pairs={{8,0},{12,4},{16,24},{20,28},{9,1},{13,5},{17,25},{21,29},{10,2},{... | collective-permute-start | bytes 4915208 | tf_op jit(solution)/shard_map/ppermute | solution.py:238
  53.0 90.8 %collective-permute-start.3 = (f32[640,640]{1,0:T(8,128)}, f32[640,640]{1,0:T(8,128)}, u32[]{:S(2)}, u32[]{:S(2)}) collective-permute-start(f32[640,640]{1,0:T(8,128)} %collective-permute-done.1.refs_3_), channel_id=1, source_target_pairs={{8,16},{12,20},{16,8},{20,12},{9,17},{13,21},{17,9},{21,13},{10,18... | collective-permute-start | bytes 4915208 | tf_op jit(solution)/shard_map/ppermute | solution.py:238
  84.9 27.6 %collective-permute-start.4 = (f32[320,640]{1,0:T(8,128)}, f32[320,640]{1,0:T(8,128)}, u32[]{:S(2)}, u32[]{:S(2)}) collective-permute-start(f32[320,640]{1,0:T(8,128)} %slice.164), channel_id=1, source_target_pairs={{0,4},{4,0},{8,12},{12,8},{16,20},{20,16},{24,28},{28,24},{1,5},{5... | collective-permute-start | bytes 2457608 | tf_op jit(solution)/shard_map/ppermute | solution.py:238
  107.2 47.9 %collective-permute-start.13 = (f32[640,640]{1,0:T(8,128)}, f32[640,640]{1,0:T(8,128)}, u32[]{:S(2)}, u32[]{:S(2)}) collective-permute-start(f32[640,640]{1,0:T(8,128)} %collective-permute-done.8), channel_id=1, source_target_pairs={{8,0},{12,4},{16,24},{20,28},{9,1},{13,5},{17,25},{21,29},{10,2},{... | collective-permute-start | bytes 4915208 | tf_op jit(solution)/shard_map/ppermute | solution.py:238
  108.5 70.4 %collective-permute-start.14 = (f32[640,640]{1,0:T(8,128)}, f32[640,640]{1,0:T(8,128)}, u32[]{:S(2)}, u32[]{:S(2)}) collective-permute-start(f32[640,640]{1,0:T(8,128)} %collective-permute-done.7.refs_3_), channel_id=1, source_target_pairs={{8,16},{12,20},{16,8},{20,12},{9,17},{13,21},{17,9},{21,13},{10,18... | collective-permute-start | bytes 4915208 | tf_op jit(solution)/shard_map/ppermute | solution.py:238
  112.5 32.9 %collective-permute-start.12 = (f32[320,640]{1,0:T(8,128)}, f32[320,640]{1,0:T(8,128)S(1)}, u32[]{:S(2)}, u32[]{:S(2)}) collective-permute-start(f32[320,640]{1,0:T(8,128)} %slice.167), channel_id=1, source_target_pairs={{0,4},{4,0},{8,12},{12,8},{16,20},{20,16},{24,28},{28,24},{1,5},{5... | collective-permute-start | bytes 2457608 | tf_op jit(solution)/shard_map/ppermute | solution.py:238
  120.0 63.0 %collective-permute-start.15 = (f32[640,512]{1,0:T(8,128)}, f32[640,512]{1,0:T(8,128)}, u32[]{:S(2)}, u32[]{:S(2)}) collective-permute-start(f32[640,512]{1,0:T(8,128)} %get-tuple-element.204), channel_id=1, source_target_pairs={{0,2},{1,3},{2,0},{3,1},{4,6},{5,7},{6,4},{7,5},{8,10},{9,11},{10,... | collective-permute-start | bytes 3932168 | tf_op jit(solution)/shard_map/ppermute | solution.py:329
  143.8 64.2 %collective-permute-start.10 = (f32[640,640]{1,0:T(8,128)}, f32[640,640]{1,0:T(8,128)}, u32[]{:S(2)}, u32[]{:S(2)}) collective-permute-start(f32[640,640]{1,0:T(8,128)} %collective-permute-done.3), channel_id=1, source_target_pairs={{8,0},{12,4},{16,24},{20,28},{9,1},{13,5},{17,25},{21,29},{10,2},{... | collective-permute-start | bytes 4915208 | tf_op jit(solution)/shard_map/ppermute | solution.py:238
  145.4 62.6 %collective-permute-start.11 = (f32[640,640]{1,0:T(8,128)S(1)}, f32[640,640]{1,0:T(8,128)}, u32[]{:S(2)}, u32[]{:S(2)}) collective-permute-start(f32[640,640]{1,0:T(8,128)S(1)} %broadcast_select_fusion.3.refs_4_), channel_id=1, source_target_pairs={{0,4},{4,0},{8,12},{12,8},{16,20},{20,16},{24,28},{28,24},{1,5},{5... | collective-permute-start | bytes 4915208 | tf_op jit(solution)/shard_map/ppermute | solution.py:238
  155.1 30.7 %collective-permute-start.16 = (f32[640,512]{1,0:T(8,128)}, f32[640,512]{1,0:T(8,128)}, u32[]{:S(2)}, u32[]{:S(2)}) collective-permute-start(f32[640,512]{1,0:T(8,128)} %collective-permute-done.9), channel_id=1, source_target_pairs={{0,2},{1,3},{2,0},{3,1},{4,6},{5,7},{6,4},{7,5},{8,10},{9,11},{10,... | collective-permute-start | bytes 3932168 | tf_op jit(solution)/shard_map/ppermute | solution.py:329
  178.9 45.3 %collective-permute-start.19 = (f32[640,640]{1,0:T(8,128)}, f32[640,640]{1,0:T(8,128)}, u32[]{:S(2)}, u32[]{:S(2)}) collective-permute-start(f32[640,640]{1,0:T(8,128)} %collective-permute-done.14), channel_id=1, source_target_pairs={{8,0},{12,4},{16,24},{20,28},{9,1},{13,5},{17,25},{21,29},{10,2},{... | collective-permute-start | bytes 4915208 | tf_op jit(solution)/shard_map/ppermute | solution.py:238
  182.9 64.6 %collective-permute-start.20 = (f32[640,640]{1,0:T(8,128)}, f32[640,640]{1,0:T(8,128)}, u32[]{:S(2)}, u32[]{:S(2)}) collective-permute-start(f32[640,640]{1,0:T(8,128)} %broadcast_select_fusion.2.refs_4_), channel_id=1, source_target_pairs={{0,4},{4,0},{8,12},{12,8},{16,20},{20,16},{24,28},{28,24},{1,5},{5... | collective-permute-start | bytes 4915208 | tf_op jit(solution)/shard_map/ppermute | solution.py:238
  209.6 74.7 %collective-permute-start.18 = (f32[640,640]{1,0:T(8,128)S(1)}, f32[640,640]{1,0:T(8,128)}, u32[]{:S(2)}, u32[]{:S(2)}) collective-permute-start(f32[640,640]{1,0:T(8,128)S(1)} %broadcast_select_fusion.1.refs_3_), channel_id=1, source_target_pairs={{0,4},{4,0},{8,12},{12,8},{16,20},{20,16},{24,28},{28,24},{1,5},{5... | collective-permute-start | bytes 4915208 | tf_op jit(solution)/shard_map/ppermute | solution.py:238
  247.5 60.0 %collective-permute-start.22 = (f32[640,640]{1,0:T(8,128)S(1)}, f32[640,640]{1,0:T(8,128)}, u32[]{:S(2)}, u32[]{:S(2)}) collective-permute-start(f32[640,640]{1,0:T(8,128)S(1)} %broadcast_select_fusion.refs_3_), channel_id=1, source_target_pairs={{0,4},{4,0},{8,12},{12,8},{16,20},{20,16},{24,28},{28,24},{1,5},{5... | collective-permute-start | bytes 4915208 | tf_op jit(solution)/shard_map/ppermute | solution.py:238
  250.0 34.2 %collective-permute-start.17 = (f32[320,640]{1,0:T(8,128)}, f32[320,640]{1,0:T(8,128)}, u32[]{:S(2)}, u32[]{:S(2)}) collective-permute-start(f32[320,640]{1,0:T(8,128)} %slice.163), channel_id=1, source_target_pairs={{0,8},{4,12},{8,0},{12,4},{16,24},{20,28},{24,16},{28,20},{1,9},{5... | collective-permute-start | bytes 2457608 | tf_op jit(solution)/shard_map/ppermute | solution.py:238
  252.1 55.5 %collective-permute-start.21 = (f32[320,640]{1,0:T(8,128)}, f32[320,640]{1,0:T(8,128)}, u32[]{:S(2)}, u32[]{:S(2)}) collective-permute-start(f32[320,640]{1,0:T(8,128)} %slice.168), channel_id=1, source_target_pairs={{0,8},{4,12},{8,0},{12,4},{16,24},{20,28},{24,16},{28,20},{1,9},{5... | collective-permute-start | bytes 2457608 | tf_op jit(solution)/shard_map/ppermute | solution.py:238
  307.6 31.0 %collective-permute-start.23 = (f32[1280,640]{1,0:T(8,128)}, f32[1280,640]{1,0:T(8,128)}, u32[]{:S(2)}, u32[]{:S(2)}) collective-permute-start(f32[1280,640]{1,0:T(8,128)} %get-tuple-element.101), channel_id=1, source_target_pairs={{0,1},{1,0},{2,3},{3,2},{4,5},{5,4},{6,7},{7,6},{8,9},{9,8},{10,11... | collective-permute-start | bytes 9830408 | tf_op jit(solution)/shard_map/ppermute | solution.py:283
  307.7 27.2 %collective-permute-start.26 = (f32[640,256]{1,0:T(8,128)S(1)}, f32[640,256]{1,0:T(8,128)S(1)}, u32[]{:S(2)}, u32[]{:S(2)}) collective-permute-start(f32[640,256]{1,0:T(8,128)S(1)} %copy-done), channel_id=1, source_target_pairs={{8,16},{12,20},{16,8},{20,12},{9,17},{13,21},{17,9},{21,13},{10,18... | collective-permute-start | bytes 1966088 | tf_op jit(solution)/shard_map/ppermute | solution.py:238
  308.4 26.5 %collective-permute-start.25 = (f32[640,256]{1,0:T(8,128)S(1)}, f32[640,256]{1,0:T(8,128)S(1)}, u32[]{:S(2)}, u32[]{:S(2)}) collective-permute-start(f32[640,256]{1,0:T(8,128)S(1)} %copy-done), channel_id=1, source_target_pairs={{0,8},{4,12},{8,0},{12,4},{16,24},{20,28},{24,16},{28,20},{1,9},{5... | collective-permute-start | bytes 1966088 | tf_op jit(solution)/shard_map/ppermute | solution.py:238
  311.1 23.8 %collective-permute-start.24 = (f32[640,256]{1,0:T(8,128)S(1)}, f32[640,256]{1,0:T(8,128)S(1)}, u32[]{:S(2)}, u32[]{:S(2)}) collective-permute-start(f32[640,256]{1,0:T(8,128)S(1)} %copy-done), channel_id=1, source_target_pairs={{0,4},{4,0},{8,12},{12,8},{16,20},{20,16},{24,28},{28,24},{1,5},{5... | collective-permute-start | bytes 1966088 | tf_op jit(solution)/shard_map/ppermute | solution.py:238
  334.9 22.8 %collective-permute-start.28 = (f32[1280,640]{1,0:T(8,128)}, f32[1280,640]{1,0:T(8,128)}, u32[]{:S(2)}, u32[]{:S(2)}) collective-permute-start(f32[1280,640]{1,0:T(8,128)} %get-tuple-element.108), channel_id=1, source_target_pairs={{0,1},{1,0},{2,3},{3,2},{4,5},{5,4},{6,7},{7,6},{8,9},{9,8},{10,11... | collective-permute-start | bytes 9830408 | tf_op jit(solution)/shard_map/ppermute | solution.py:283
  335.0 20.3 %collective-permute-start.30 = (f32[640,256]{1,0:T(8,128)S(1)}, f32[640,256]{1,0:T(8,128)S(1)}, u32[]{:S(2)}, u32[]{:S(2)}) collective-permute-start(f32[640,256]{1,0:T(8,128)S(1)} %collective-permute-done.25.refs_3_), channel_id=1, source_target_pairs={{8,16},{12,20},{16,8},{20,12},{9,17},{13,21},{17,9},{21,13},{10,18... | collective-permute-start | bytes 1966088 | tf_op jit(solution)/shard_map/ppermute | solution.py:238
  343.2 46.5 %collective-permute-start.27 = (f32[640,640]{1,0:T(8,128)}, f32[640,640]{1,0:T(8,128)}, u32[]{:S(2)}, u32[]{:S(2)}) collective-permute-start(f32[640,640]{1,0:T(8,128)} %slice_bitcast_fusion.2), channel_id=1, source_target_pairs={{0,2},{1,3},{2,0},{3,1},{4,6},{5,7},{6,4},{7,5},{8,10},{9,11},{10,... | collective-permute-start | bytes 4915208 | tf_op jit(solution)/shard_map/ppermute | solution.py:283
  374.7 41.8 %collective-permute-start.29 = (f32[640,640]{1,0:T(8,128)}, f32[640,640]{1,0:T(8,128)}, u32[]{:S(2)}, u32[]{:S(2)}) collective-permute-start(f32[640,640]{1,0:T(8,128)} %slice_bitcast_fusion), channel_id=1, source_target_pairs={{0,2},{1,3},{2,0},{3,1},{4,6},{5,7},{6,4},{7,5},{8,10},{9,11},{10,... | collective-permute-start | bytes 4915208 | tf_op jit(solution)/shard_map/ppermute | solution.py:283
  403.8 21.9 %collective-permute-start.37 = (f32[1280,256]{1,0:T(8,128)S(1)}, f32[1280,256]{1,0:T(8,128)S(1)}, u32[]{:S(2)}, u32[]{:S(2)}) collective-permute-start(f32[1280,256]{1,0:T(8,128)S(1)} %copy-done.21), channel_id=1, source_target_pairs={{0,1},{1,0},{2,3},{3,2},{4,5},{5,4},{6,7},{7,6},{8,9},{9,8},{10,11... | collective-permute-start | bytes 3932168 | tf_op jit(solution)/shard_map/ppermute | solution.py:283
  430.8 22.5 %collective-permute-start.40 = (f32[1,2,512,128]{3,2,1,0:T(8,128)S(1)}, f32[1,2,512,128]{3,2,1,0:T(8,128)S(1)}, u32[]{:S(2)}, u32[]{:S(2)}) collective-permute-start(f32[1,2,512,128]{3,2,1,0:T(8,128)S(1)} %fusion.24), channel_id=1, source_target_pairs={{0,2},{1,3},{2,0},{3,1},{4,6},{5,7},{6,4},{7,5},{8,10},{9,11},{10,... | collective-permute-start | bytes 1572872 | tf_op jit(solution)/shard_map/ppermute | solution.py:302
  (49 other events, 558.3 us)

commit v2 on v1

--- a/solution.py
+++ b/solution.py
@@ -192,7 +192,6 @@
 def fast_on_device(n_prow, n_pcol, ainv, panels, ancestors, dinv):
     sups, depth, wide = panels.shape
     length = n_prow // 2
-    half = depth // 2
     own_p = lax.axis_index("prow")
     own_c = lax.axis_index("pcol")
     place, side = own_p // 2, own_p % 2
@@ -249,7 +248,7 @@
                 new.append(group.over)
             here.append(group.first)
         elif step == 1:
-            there.append([send(here[1][:half], side_pairs)])
+            there.append([send(here[1], side_pairs)])
             new.append(there[1][0])
             if length >= 4:
                 hops2 = chain_hops(length, 2)
@@ -263,60 +262,65 @@
             new += [inward, there[2][0]]
             here.append(jnp.where(at_edge, group.over2, inward))
         elif step == 3:
-            second = send(there[0][0][half:], hops1)
-            there[1].append(second)
             there.append([send(here[3], side_pairs)])
-            new += [second, there[3][0]]
+            new.append(there[3][0])
         return new
 
     at_edge = jnp.logical_or(place == length // 2 - 1, place == length // 2)
 
     def items(group, step):
         here, there = group.here, group.there
-        wanted = [((0, 0), (1, 0)), ((0, 1), (0, 2)), ((0, 3), (1, 2)), ((1, 3), (1, 1))][step]
+        if group is last_group:
+            plan = [((0, 0), (1, 0)), ((0, 1), (0, 2), (1, 1)), (), ((0, 3), (1, 2), (1, 3))]
+        else:
+            plan = [((0, 0), (1, 0)), ((0, 1), (0, 2)), ((0, 3), (1, 1)), ((1, 3), (1, 2))]
+        wanted = plan[step]
         return [(there[k], other_side[k]) if over else ([here[k]], same_side[k]) for over, k in wanted]
 
-    def sum_rows(kept, away, tick):
-        for index, bit in enumerate(pcol_bits):
-            if tick + 1 + index < len(arrived):
-                away = follow(away, arrived[tick + 1 + index])
+    def sum_rows(group, kept, away, tick):
+        for bit in pcol_bits:
+            if bit == 1 and group is second_group:
+                away = follow(away, arrived[tick + 1])
+            if group is last_group and bit == pcol_bits[-1]:
+                away = follow(away, row_sums[-1:])
             received = lax.ppermute(away, "pcol", pcol_pairs(bit))
+            if kept.shape[0] == depth:
+                if group is first_group:
+                    want(tick + 4, received)
+                row_sums.append(received)
+                return kept, received, away
             total = kept + received
-            if total.shape[0] == depth:
-                want(tick + 5, received)
-                return total
             blocks = total.reshape(total.shape[0] // (2 * depth), 2, depth, total.shape[1])
             kept = blocks[:, 0].reshape(-1, total.shape[1])
             away = blocks[:, 1].reshape(-1, total.shape[1])
-            want(tick + 2 if tick + 2 < len(ticks) else tick + 1, away)
-
-    def sum_diagonal(terms, start, tick):
-        width = terms.shape[2]
-        count = width // cols
-        low_bits = [bit for bit in pcol_bits if bit < count]
-        blocks = {
-            q: lax.dynamic_slice_in_dim(terms, ((own_c ^ q) % count) * cols, cols, 2) for q in range(count)
-        }
-        for bit in low_bits:
+            want(tick + 2, away)
+
+    def sum_diagonal(terms, first_bits):
+        blocks = {q: lax.dynamic_slice_in_dim(terms, (own_c ^ q) * cols, cols, 2) for q in range(n_pcol)}
+
+        def halve_columns(blocks, bit):
             away = [q for q in sorted(blocks) if q & bit]
             moved = lax.ppermute(jnp.stack([blocks[q] for q in away]), "pcol", pcol_pairs(bit))
-            want(tick, moved)
-            tick += 1
-            blocks = {q ^ bit: blocks[q ^ bit] + moved[k] for k, q in enumerate(away)}
-        value = blocks[0].reshape(terms.shape[0], n_prow, rows_own, cols)
+            return {q ^ bit: blocks[q ^ bit] + moved[k] for k, q in enumerate(away)}
+
+        for bit in first_bits:
+            blocks = halve_columns(blocks, bit)
+            sent.append(blocks[0])
+        order = sorted(blocks)
+        value = jnp.stack([blocks[q] for q in order]).reshape(len(order) * terms.shape[0], n_prow, rows_own, cols)
         for bit in prow_bits:
             paired = value.reshape(value.shape[0], value.shape[1] // 2, 2, rows_own, cols)
             mine = (own_p // bit) % 2
             keep = lax.dynamic_index_in_dim(paired, mine, 2, keepdims=False)
             send = lax.dynamic_index_in_dim(paired, 1 - mine, 2, keepdims=False)
             value = keep + lax.ppermute(send, "prow", prow_pairs(bit))
-            want(tick, value)
-            tick += 1
-        value = value[:, 0]
+            sent.append(value)
+        value = value.reshape(len(order), terms.shape[0], rows_own, cols)
+        blocks = {q: value[k] for k, q in enumerate(order)}
         for bit in pcol_bits:
-            if bit not in low_bits:
-                value = value + lax.ppermute(value, "pcol", pcol_pairs(bit))
-        return value
+            if bit not in first_bits:
+                blocks = halve_columns(blocks, bit)
+        return blocks[0]
 
     def transposed_product(left, right):
         return lax.dot_general(
@@ -324,63 +328,76 @@
             preferred_element_type=jnp.float32,
         )
 
+    row_sums = []
     near = [masked[-1]]
-    for index, bit in enumerate(pcol_bits):
-        moved = [lax.ppermute(value, "pcol", pcol_pairs(bit)) for value in near]
-        want(1 + 2 * index, *moved)
-        near += moved
-    near_kept = jnp.concatenate(near[0::2], axis=0)
-    near_away = jnp.concatenate(near[1::2], axis=0)
+
+    def exchange_near(bit, tick):
+        after = arrived[tick - 1]
+        moved = [lax.ppermute(follow(value, after), "pcol", pcol_pairs(bit)) for value in near]
+        want(tick + 2, *moved)
+        near.extend(moved)
 
     ticks = [(group, step) for step in range(4) for group in (first_group, second_group)]
     ticks += [(last_group, step) for step in range(4)]
     turns = 8
     arrived, tokens = [], []
     parts = [[] for _ in range(sups)]
-    diag = [[] for _ in range(sups)]
+    last_terms = []
 
     def start(k):
         group, step = ticks[k]
-        lead = 2 if k <= turns else 1
-        after = (arrived[k - lead] if k >= lead else []) + ([tokens[k - lead - 1]] if k > lead else [])
+        if k <= turns:
+            after = arrived[k - 2] + [tokens[k - 2]] if k >= 2 else []
+        else:
+            after = arrived[k - 1] + [tokens[k - 2]]
         arrived.append(moves(group, step, after))
 
-    started = 0
+    start(0)
+    start(1)
     for k, (group, step) in enumerate(ticks):
-        while started < len(ticks) and started <= (k + 2 if k + 2 <= turns else max(k + 1, turns)):
-            start(started)
-            started += 1
-        if k == len(ticks) - 1:
-            products = [
-                transposed_product(masked[m], follow(jnp.concatenate(parts[m], axis=1), tokens[-1:]))
-                for m in range(sups - 1)
-            ]
-            for m, value in enumerate(sum_diagonal(jnp.stack(products), 0, k + 1)):
-                diag[m].append(value)
+        if 1 <= k <= len(pcol_bits):
+            exchange_near(pcol_bits[k - 1], k)
         chosen = items(group, step)
+        if not chosen:
+            want(k + 1, *due.get(k, []))
+            start(k + 1)
+            continue
         last = step == 3
         *sums, token = add_products(
             ainv, own_c, [c[0] for c in chosen], [c[1] for c in chosen], group.running, depth,
-            parted=last, after=arrived[k] + (tokens[-1:]) + due.get(k, []),
+            parted=last, after=arrived[k] + tokens[-1:] + due.get(k, []),
         )
         tokens.append(token)
+        if k + 2 <= turns:
+            start(k + 2)
+        elif k + 2 < len(ticks) - 1:
+            start(k + 2)
         if not last:
             group.running = sums[0]
             continue
         kept, away = sums
         if group is last_group:
-            diag[-1].append(-(transposed_product(near_kept, kept) + transposed_product(near_away, away)))
-        summed = sum_rows(kept, away, k)
+            near_kept = jnp.concatenate(near[0::2], axis=0)
+            near_away = jnp.concatenate(near[1::2], axis=0)
+            last_terms.append(-(transposed_product(near_kept, kept) + transposed_product(near_away, away)))
+        own_sum, other_sum, last_sent = sum_rows(group, kept, away, k)
+        if group is last_group:
+            sent = [last_sent]
+            last_diag = sum_diagonal(jnp.concatenate(last_terms, axis=1)[None], pcol_bits[:1])
+            others_after = sent[:2]
+            other_sum = follow(other_sum, sent[2:3])
+        summed = own_sum + other_sum
         at = 0
         for member, _, width in group.pieces:
             part = -(flags[member][:, None] * summed[:, at : at + width])
             at += width
             parts[member].append(part)
             if member == sups - 1 and group is not last_group:
-                diag[-1].append(transposed_product(masked[member], follow(part, tokens[-1:])))
-    u_panel = jnp.stack([jnp.concatenate(part, axis=1) for part in parts])
-    diag[-1] = [sum_diagonal(jnp.concatenate(diag[-1], axis=1)[None], 0, len(ticks))[0]]
-    return u_panel, dinv - jnp.stack([found[0] for found in diag])
+                last_terms.append(transposed_product(masked[member], follow(part, tokens[-1:])))
+    u_whole = [jnp.concatenate(part, axis=1) for part in parts]
+    terms = [transposed_product(masked[m], follow(u_whole[m], others_after)) for m in range(sups - 1)]
+    other_diag = sum_diagonal(jnp.stack(terms), pcol_bits[:1])
+    return jnp.stack(u_whole), dinv - jnp.concatenate([other_diag, last_diag], axis=0)
 
 
 def solution(mesh):

time: 487 us -> 475 us (0.975)
  Pallas kernels: 227 us -> 216 us
  other arithmetic: 25.5 us -> 35.8 us
  local copies, waits for them, and re-layouts: 21.3 us -> 15.2 us
    ppermute x6, waiting for transfers between devices: 23 us -> 0.02 us  [sum_rows(): received = lax.ppermute(away, 'pcol', pcol_pairs(bit))]
    ppermute x30 -> x27, waiting for transfers between devices: 87.2 us -> 100 us  [moves(): lax.ppermute(follow(value, after), 'prow', pairs)]
    ppermute x6, waiting for transfers between devices: 8.37 us -> 20.2 us  [sum_diagonal(): value = keep + lax.ppermute(send, 'prow', prow_pairs(bit))]
    pallas_call x12 -> x11, Pallas kernels: 227 us -> 216 us  [add_products(): pl.pallas_call(functools.partial(product_kernel, tuple((len(item) for ite...]
    slice x6 -> x2, local copies, waits for them, and re-layouts: 7.34 us -> 0.01 us  [sum_diagonal(): blocks = {q: value[k] for k, q in enumerate(order)}]
    ppermute x30 -> x27, starting transfers between devices: 43 us -> 43.9 us  [moves(): lax.ppermute(follow(value, after), 'prow', pairs)]
  transfers between devices with their start and end apart: 49 -> 46, of which waited for: 18 -> 18; matrix products, arithmetic and copies ran while one was open for 10% -> 11% of each run, Pallas kernels for 47% -> 46%
where the time goes in v2:
time: 475 us; the launch traced here: 468 us
  Pallas kernels  216 us (45%)
  waiting for transfers between devices  127 us (27%)
  starting transfers between devices  60.3 us (13%)
  other arithmetic  35.8 us (8%)
  local copies, waits for them, and re-layouts  15.2 us (3%)
  matrix products  10.1 us (2%)
    pallas_call x11, Pallas kernels, add_products(): pl.pallas_call(functools.partial(product_kernel, tuple((len(item) for ite...  216 us
    ppermute x27, waiting for transfers between devices, moves(): lax.ppermute(follow(value, after), 'prow', pairs)  100 us
    ppermute x27, starting transfers between devices, moves(): lax.ppermute(follow(value, after), 'prow', pairs)  43.9 us
    ppermute x6, waiting for transfers between devices, sum_diagonal(): value = keep + lax.ppermute(send, 'prow', prow_pairs(bit))  20.2 us
    dot_general x5, matrix products, transposed_product(): lax.dot_general(left, right, (((0,), (0,)), ((), ())), precision=lax.Prec...  10.1 us
  transfers between devices with their start and end apart: 46, of which 18 were waited for; matrix products, arithmetic and copies ran while one was open for 11% of the time, Pallas kernels for 46%

profile of v2, /device:TPU:0, one launch (start us, length us, event | category | flops | bytes accessed | tf_op | source)
XLA Modules:
  0.0 468.1 jit_solution(11704967274751990824)
XLA Ops:
  6.2 3.0 collective-permute-start.1
  9.2 4.3 collective-permute-start
  18.9 27.1 %collective-permute-done.1.refs_4_ = f32[640,640]{1,0:T(8,128)} collective-permute-done((f32[640,640]{1,0:T(8,128)S(1)}, f32[640,640]{1,0:T(8,128)}, u32[]{:S(2)}, u32[]{:S(2)}) %collective-permute-start.1) | collective-permute-done | bytes 1638432 | tf_op jit(solution)/shard_map/ppermute | solution.py:237
  46.0 4.4 collective-permute-done.refs_3_
  50.3 20.7 %shard_map.95 = (f32[2560,640]{1,0:T(8,128)}, f32[8,128]{1,0:T(8,128)}) custom-call(s32[3]{0:T(128)S(1)} %pad_add_fusion.1.refs_0_, f32[2560,5120]{1,0:T(8,128)} %refs_3_.3, f32[2560,5120]{1,0:T(8,128)} %refs_3_.3, f32[640,640]{1,0:T(8,128)S(1)} %pad_maximum_fusion.1.refs_3_, f32[640,640]{1,0:T(8,128)} %collective-permute-done.1.refs_4_), custom_call_target="tpu_custom_call" | custom-call | flops 1 | bytes 1 | tf_op jit(solution)/shard_map/pallas_call | solution.py:134
  74.7 9.3 %collective-permute-done.7.refs_3_ = f32[640,640]{1,0:T(8,128)} collective-permute-done((f32[640,640]{1,0:T(8,128)S(1)}, f32[640,640]{1,0:T(8,128)}, u32[]{:S(2)}, u32[]{:S(2)}) %collective-permute-start.7) | collective-permute-done | bytes 1638432 | tf_op jit(solution)/shard_map/ppermute | solution.py:237
  84.0 20.7 %shard_map.96 = (f32[2560,640]{1,0:T(8,128)}, f32[8,128]{1,0:T(8,128)}) custom-call(s32[3]{0:T(128)S(1)} %pad_add_fusion.1.refs_0_, f32[2560,5120]{1,0:T(8,128)} %refs_3_.3, f32[2560,5120]{1,0:T(8,128)} %refs_3_.3, f32[640,640]{1,0:T(8,128)S(1)} %pad_maximum_fusion.2.refs_3_, f32[640,640]{1,0:T(8,128)} %collective-permute-done.6.refs_4_), custom_call_target="tpu_custom_call" | custom-call | flops 1 | bytes 1 | tf_op jit(solution)/shard_map/pallas_call | solution.py:134
  106.5 8.7 %collective-permute-done.4.refs_4_ = f32[640,640]{1,0:T(8,128)S(1)} collective-permute-done((f32[640,640]{1,0:T(8,128)}, f32[640,640]{1,0:T(8,128)S(1)}, u32[]{:S(2)}, u32[]{:S(2)}) %collective-permute-start.4) | collective-permute-done | bytes 1638432 | tf_op jit(solution)/shard_map/ppermute | solution.py:237
  124.5 2.8 broadcast_select_fusion.3.refs_4_
  127.3 23.2 %shard_map.97 = (f32[2560,640]{1,0:T(8,128)}, f32[8,128]{1,0:T(8,128)}) custom-call(s32[3]{0:T(128)S(1)} %pad_add_fusion.2.refs_0_, f32[2560,5120]{1,0:T(8,128)} %refs_3_.3, f32[2560,5120]{1,0:T(8,128)} %refs_3_.3, f32[640,640]{1,0:T(8,128)} %collective-permute-done.refs_3_, ...), custom_call_target="tpu_custom_call", output_to_operand_aliasing={{0}: (5, {})} | custom-call | flops 1 | bytes 1 | tf_op jit(solution)/shard_map/pallas_call | solution.py:134
  154.9 3.1 collective-permute-done.12
  160.7 22.2 %shard_map.98 = (f32[2560,640]{1,0:T(8,128)}, f32[8,128]{1,0:T(8,128)}) custom-call(s32[3]{0:T(128)S(1)} %pad_add_fusion.2.refs_0_, f32[2560,5120]{1,0:T(8,128)} %refs_3_.3, f32[2560,5120]{1,0:T(8,128)} %refs_3_.3, f32[640,640]{1,0:T(8,128)} %collective-permute-done.7.refs_3_, ...), custom_call_target="tpu_custom_call", output_to_operand_aliasing={{0}: (5, {})} | custom-call | flops 1 | bytes 1 | tf_op jit(solution)/shard_map/pallas_call | solution.py:134
  186.3 8.5 %collective-permute-done.9 = f32[640,640]{1,0:T(8,128)} collective-permute-done((f32[640,640]{1,0:T(8,128)}, f32[640,640]{1,0:T(8,128)}, u32[]{:S(2)}, u32[]{:S(2)}) %collective-permute-start.9) | collective-permute-done | bytes 1638432 | tf_op jit(solution)/shard_map/ppermute | solution.py:237
  196.5 21.9 %shard_map.99 = (f32[2560,640]{1,0:T(8,128)}, f32[8,128]{1,0:T(8,128)}) custom-call(s32[3]{0:T(128)S(1)} %pad_add_fusion.3.refs_0_, f32[2560,5120]{1,0:T(8,128)} %refs_3_.3, f32[2560,5120]{1,0:T(8,128)} %refs_3_.3, f32[640,640]{1,0:T(8,128)S(1)} %broadcast_select_fusion.2.refs_3_, f32[640,640]{1,0:T(8,128)} %copy-done.29, ...), custom_call_target="tpu_custom_call", output_to_operand_aliasing={{0}: (5, {})} | custom-call | flops 1 | bytes 1 | tf_op jit(solution)/shard_map/pallas_call | solution.py:134
  218.7 8.3 %collective-permute-done.18 = f32[640,640]{1,0:T(8,128)} collective-permute-done((f32[640,640]{1,0:T(8,128)}, f32[640,640]{1,0:T(8,128)}, u32[]{:S(2)}, u32[]{:S(2)}) %collective-permute-start.18) | collective-permute-done | bytes 1638432 | tf_op jit(solution)/shard_map/ppermute | solution.py:237
  228.7 21.7 %shard_map.100 = (f32[2560,640]{1,0:T(8,128)}, f32[8,128]{1,0:T(8,128)}) custom-call(s32[3]{0:T(128)S(1)} %pad_add_fusion.3.refs_0_, f32[2560,5120]{1,0:T(8,128)} %refs_3_.3, f32[2560,5120]{1,0:T(8,128)} %refs_3_.3, f32[640,640]{1,0:T(8,128)S(1)} %broadcast_select_fusion.refs_3_, ...), custom_call_target="tpu_custom_call", output_to_operand_aliasing={{0}: (5, {})} | custom-call | flops 1 | bytes 1 | tf_op jit(solution)/shard_map/pallas_call | solution.py:134
  251.0 10.0 %collective-permute-done.17.refs_3_ = f32[640,640]{1,0:T(8,128)} collective-permute-done((f32[640,640]{1,0:T(8,128)S(1)}, f32[640,640]{1,0:T(8,128)}, u32[]{:S(2)}, u32[]{:S(2)}) %collective-permute-start.17) | collective-permute-done | bytes 1638432 | tf_op jit(solution)/shard_map/ppermute | solution.py:237
  260.9 23.3 %shard_map.101 = (f32[1280,640]{1,0:T(8,128)}, f32[1280,640]{1,0:T(8,128)}, f32[8,128]{1,0:T(8,128)}) custom-call(s32[3]{0:T(128)S(1)} %pad_add_fusion.refs_0_, f32[2560,5120]{1,0:T(8,128)} %refs_3_.3, f32[2560,5120]{1,0:T(8,128)} %refs_3_.3, f32[640,640]{1,0:T(8,128)} %collective-permute-done.17.refs_3_, f32[640,640]{1,0:T(8,128)} %collective-permute-done.10.refs_4_, ...), custom_call_target="tpu_custom_call" | custom-call | flops 1 | bytes 1 | tf_op jit(solution)/shard_map/pallas_call | solution.py:134
  285.2 9.9 %collective-permute-start.24 = (f32[640,256]{1,0:T(8,128)S(1)}, f32[640,256]{1,0:T(8,128)S(1)}, u32[]{:S(2)}, u32[]{:S(2)}) collective-permute-start(f32[640,256]{1,0:T(8,128)S(1)} %copy-done), channel_id=1, source_target_pairs={{0,8},{4,12},{8,0},{12,4},{16,24},{20,28},{24,16},{28,20},{1,9},{5... | collective-permute-start | bytes 1966088 | tf_op jit(solution)/shard_map/ppermute | solution.py:237
  295.9 23.6 %shard_map.102 = (f32[1280,640]{1,0:T(8,128)}, f32[1280,640]{1,0:T(8,128)}, f32[8,128]{1,0:T(8,128)}) custom-call(s32[3]{0:T(128)S(1)} %pad_add_fusion.refs_0_, f32[2560,5120]{1,0:T(8,128)} %refs_3_.3, f32[2560,5120]{1,0:T(8,128)} %refs_3_.3, f32[640,640]{1,0:T(8,128)} %collective-permute-done.22.refs_3_, f32[640,640]{1,0:T(8,128)} %collective-permute-done.19.refs_4_, ...), custom_call_target="tpu_custom_call" | custom-call | flops 1 | bytes 1 | tf_op jit(solution)/shard_map/pallas_call | solution.py:134
  328.2 10.5 %shard_map.103 = (f32[2560,256]{1,0:T(8,128)}, f32[8,128]{1,0:T(8,128)}) custom-call(s32[3]{0:T(128)S(1)} %copy-done.2, f32[2560,5120]{1,0:T(8,128)} %refs_3_.3, f32[2560,5120]{1,0:T(8,128)} %refs_3_.3, f32[640,256]{1,0:T(8,128)S(1)} %copy-done, f32[640,256]{1,0:T(8,128)S(1)} %collective-permute-done.23.refs_4_), custom_call_target="tpu_custom_call" | custom-call | flops 1 | bytes 1 | tf_op jit(solution)/shard_map/pallas_call | solution.py:134
  338.7 5.5 %collective-permute-done.30 = f32[640,256]{1,0:T(8,128)S(1)} collective-permute-done((f32[640,256]{1,0:T(8,128)S(1)}, f32[640,256]{1,0:T(8,128)S(1)}, u32[]{:S(2)}, u32[]{:S(2)}) %collective-permute-start.30) | collective-permute-done | bytes 655392 | tf_op jit(solution)/shard_map/ppermute | solution.py:237
  351.8 13.9 %shard_map.104 = (f32[2560,256]{1,0:T(8,128)}, f32[8,128]{1,0:T(8,128)}) custom-call(s32[4]{0:T(128)S(1)} %pad_add_fusion.5.refs_0_, f32[2560,5120]{1,0:T(8,128)} %refs_3_.3, f32[2560,5120]{1,0:T(8,128)} %refs_3_.3, f32[2560,5120]{1,0:T(8,128)} %refs_3_.3, f32[640,256]{1,0:T(8,128)S(1)} %collective-permute-done.24.refs_4_, ...), custom_call_target="tpu_custom_call", output_to_operand_aliasing={{0}: (7, {})} | custom-call | flops 1 | bytes 1 | tf_op jit(solution)/shard_map/pallas_call | solution.py:134
  366.9 14.7 %collective-permute-done.33.refs_6_ = f32[640,256]{1,0:T(8,128)S(1)} collective-permute-done((f32[640,256]{1,0:T(8,128)S(1)}, f32[640,256]{1,0:T(8,128)S(1)}, u32[]{:S(2)}, u32[]{:S(2)}) %collective-permute-start.33) | collective-permute-done | bytes 655392 | tf_op jit(solution)/shard_map/ppermute | solution.py:237
  381.7 14.5 %shard_map.105 = (f32[1280,256]{1,0:T(8,128)}, f32[1280,256]{1,0:T(8,128)}, f32[8,128]{1,0:T(8,128)}) custom-call(s32[4]{0:T(128)S(1)} %pad_add_fusion.4.refs_0_, f32[2560,5120]{1,0:T(8,128)} %refs_3_.3, f32[2560,5120]{1,0:T(8,128)} %refs_3_.3, f32[2560,5120]{1,0:T(8,128)} %refs_3_.3, f32[640,256]{1,0:T(8,128)S(1)} %broadcast_select_fusion.5.refs_4_, ...), custom_call_target="tpu_custom_call" | custom-call | flops 1 | bytes 1 | tf_op jit(solution)/shard_map/pallas_call | solution.py:134
  396.2 3.5 fusion.4
  399.7 2.8 fusion.14
  427.0 3.7 collective-permute-done.43
  439.1 5.0 %collective-permute-done.45 = f32[1,1,64,128]{3,2,1,0:T(8,128)S(1)} collective-permute-done((f32[1,1,64,128]{3,2,1,0:T(8,128)S(1)}, f32[1,1,64,128]{3,2,1,0:T(8,128)S(1)}, u32[]{:S(2)}, u32[]{:S(2)}) %collective-permute-start.45) | collective-permute-done | bytes 32800 | tf_op jit(solution)/shard_map/ppermute | solution.py:303
  444.1 4.3 collective-permute-done.39
  449.2 6.0 %collective-permute-done.40 = f32[4,2,64,128]{3,2,1,0:T(8,128)S(1)} collective-permute-done((f32[4,2,64,128]{3,2,1,0:T(8,128)S(1)}, f32[4,2,64,128]{3,2,1,0:T(8,128)S(1)}, u32[]{:S(2)}, u32[]{:S(2)}) %collective-permute-start.40) | collective-permute-done | bytes 262176 | tf_op jit(solution)/shard_map/ppermute | solution.py:316
  457.2 5.5 %collective-permute-done.41 = f32[4,1,64,128]{3,2,1,0:T(8,128)S(1)} collective-permute-done((f32[4,1,64,128]{3,2,1,0:T(8,128)S(1)}, f32[4,1,64,128]{3,2,1,0:T(8,128)S(1)}, u32[]{:S(2)}, u32[]{:S(2)}) %collective-permute-start.41) | collective-permute-done | bytes 131104 | tf_op jit(solution)/shard_map/ppermute | solution.py:316
  (230 shorter events, 97.8 us)
Async XLA Ops:
  6.2 39.8 %collective-permute-start.1 = (f32[640,640]{1,0:T(8,128)S(1)}, f32[640,640]{1,0:T(8,128)}, u32[]{:S(2)}, u32[]{:S(2)}) collective-permute-start(f32[640,640]{1,0:T(8,128)S(1)} %pad_maximum_fusion.1.refs_3_), channel_id=1, source_target_pairs={{0,4},{4,0},{8,12},{12,8},{16,20},{20,16},{24,28},{28,24},{1,5},{5... | collective-permute-start | bytes 4915208 | tf_op jit(solution)/shard_map/ppermute | solution.py:237
  9.2 41.1 %collective-permute-start = (f32[640,640]{1,0:T(8,128)S(1)}, f32[640,640]{1,0:T(8,128)}, u32[]{:S(2)}, u32[]{:S(2)}) collective-permute-start(f32[640,640]{1,0:T(8,128)S(1)} %pad_maximum_fusion.1.refs_3_), channel_id=1, source_target_pairs={{0,8},{4,12},{8,0},{12,4},{16,24},{20,28},{24,16},{28,20},{1,9},{5... | collective-permute-start | bytes 4915208 | tf_op jit(solution)/shard_map/ppermute | solution.py:237
  14.7 58.7 %collective-permute-start.8 = (f32[640,640]{1,0:T(8,128)S(1)}, f32[640,640]{1,0:T(8,128)}, u32[]{:S(2)}, u32[]{:S(2)}) collective-permute-start(f32[640,640]{1,0:T(8,128)S(1)} %pad_maximum_fusion.2.refs_3_), channel_id=1, source_target_pairs={{8,16},{12,20},{16,8},{20,12},{9,17},{13,21},{17,9},{21,13},{10,18... | collective-permute-start | bytes 4915208 | tf_op jit(solution)/shard_map/ppermute | solution.py:237
  16.5 67.5 %collective-permute-start.7 = (f32[640,640]{1,0:T(8,128)S(1)}, f32[640,640]{1,0:T(8,128)}, u32[]{:S(2)}, u32[]{:S(2)}) collective-permute-start(f32[640,640]{1,0:T(8,128)S(1)} %pad_maximum_fusion.2.refs_3_), channel_id=1, source_target_pairs={{0,8},{4,12},{8,0},{12,4},{16,24},{20,28},{24,16},{28,20},{1,9},{5... | collective-permute-start | bytes 4915208 | tf_op jit(solution)/shard_map/ppermute | solution.py:237
  18.3 65.7 %collective-permute-start.6 = (f32[640,640]{1,0:T(8,128)S(1)}, f32[640,640]{1,0:T(8,128)}, u32[]{:S(2)}, u32[]{:S(2)}) collective-permute-start(f32[640,640]{1,0:T(8,128)S(1)} %pad_maximum_fusion.2.refs_3_), channel_id=1, source_target_pairs={{0,4},{4,0},{8,12},{12,8},{16,20},{20,16},{24,28},{28,24},{1,5},{5... | collective-permute-start | bytes 4915208 | tf_op jit(solution)/shard_map/ppermute | solution.py:237
  71.0 44.2 %collective-permute-start.4 = (f32[640,640]{1,0:T(8,128)}, f32[640,640]{1,0:T(8,128)S(1)}, u32[]{:S(2)}, u32[]{:S(2)}) collective-permute-start(f32[640,640]{1,0:T(8,128)} %collective-permute-done.refs_3_), channel_id=1, source_target_pairs={{0,4},{4,0},{8,12},{12,8},{16,20},{20,16},{24,28},{28,24},{1,5},{5... | collective-permute-start | bytes 4915208 | tf_op jit(solution)/shard_map/ppermute | solution.py:237
  71.6 45.4 %collective-permute-start.3 = (f32[640,640]{1,0:T(8,128)}, f32[640,640]{1,0:T(8,128)}, u32[]{:S(2)}, u32[]{:S(2)}) collective-permute-start(f32[640,640]{1,0:T(8,128)} %collective-permute-done.refs_3_), channel_id=1, source_target_pairs={{8,16},{12,20},{16,8},{20,12},{9,17},{13,21},{17,9},{21,13},{10,18... | collective-permute-start | bytes 4915208 | tf_op jit(solution)/shard_map/ppermute | solution.py:237
  73.4 45.9 %collective-permute-start.5 = (f32[640,640]{1,0:T(8,128)S(1)}, f32[640,640]{1,0:T(8,128)S(1)}, u32[]{:S(2)}, u32[]{:S(2)}) collective-permute-start(f32[640,640]{1,0:T(8,128)S(1)} %copy-done.27), channel_id=1, source_target_pairs={{8,0},{12,4},{16,24},{20,28},{9,1},{13,5},{17,25},{21,29},{10,2},{... | collective-permute-start | bytes 4915208 | tf_op jit(solution)/shard_map/ppermute | solution.py:237
  104.7 47.1 %collective-permute-start.13 = (f32[640,640]{1,0:T(8,128)}, f32[640,640]{1,0:T(8,128)}, u32[]{:S(2)}, u32[]{:S(2)}) collective-permute-start(f32[640,640]{1,0:T(8,128)} %collective-permute-done.7.refs_3_), channel_id=1, source_target_pairs={{8,16},{12,20},{16,8},{20,12},{9,17},{13,21},{17,9},{21,13},{10,18... | collective-permute-start | bytes 4915208 | tf_op jit(solution)/shard_map/ppermute | solution.py:237
  106.5 44.0 %collective-permute-start.14 = (f32[640,512]{1,0:T(8,128)S(1)}, f32[640,512]{1,0:T(8,128)}, u32[]{:S(2)}, u32[]{:S(2)}) collective-permute-start(f32[640,512]{1,0:T(8,128)S(1)} %copy-done.4), channel_id=1, source_target_pairs={{0,1},{1,0},{2,3},{3,2},{4,5},{5,4},{6,7},{7,6},{8,9},{9,8},{10,11... | collective-permute-start | bytes 3932168 | tf_op jit(solution)/shard_map/ppermute | solution.py:336
  115.3 38.0 %collective-permute-start.11 = (f32[640,640]{1,0:T(8,128)}, f32[640,640]{1,0:T(8,128)}, u32[]{:S(2)}, u32[]{:S(2)}) collective-permute-start(f32[640,640]{1,0:T(8,128)} %collective-permute-done.7.refs_3_), channel_id=1, source_target_pairs={{0,4},{4,0},{8,12},{12,8},{16,20},{20,16},{24,28},{28,24},{1,5},{5... | collective-permute-start | bytes 4915208 | tf_op jit(solution)/shard_map/ppermute | solution.py:237
  117.0 41.0 %collective-permute-start.12 = (f32[640,640]{1,0:T(8,128)}, f32[640,640]{1,0:T(8,128)}, u32[]{:S(2)}, u32[]{:S(2)}) collective-permute-start(f32[640,640]{1,0:T(8,128)} %collective-permute-done.8), channel_id=1, source_target_pairs={{8,0},{12,4},{16,24},{20,28},{9,1},{13,5},{17,25},{21,29},{10,2},{... | collective-permute-start | bytes 4915208 | tf_op jit(solution)/shard_map/ppermute | solution.py:237
  120.5 63.7 %collective-permute-start.15 = (f32[640,512]{1,0:T(8,128)S(1)}, f32[640,512]{1,0:T(8,128)}, u32[]{:S(2)}, u32[]{:S(2)}) collective-permute-start(f32[640,512]{1,0:T(8,128)S(1)} %copy-done.4), channel_id=1, source_target_pairs={{0,2},{1,3},{2,0},{3,1},{4,6},{5,7},{6,4},{7,5},{8,10},{9,11},{10,... | collective-permute-start | bytes 3932168 | tf_op jit(solution)/shard_map/ppermute | solution.py:336
  150.5 44.3 %collective-permute-start.9 = (f32[640,640]{1,0:T(8,128)}, f32[640,640]{1,0:T(8,128)}, u32[]{:S(2)}, u32[]{:S(2)}) collective-permute-start(f32[640,640]{1,0:T(8,128)} %collective-permute-done.3), channel_id=1, source_target_pairs={{8,0},{12,4},{16,24},{20,28},{9,1},{13,5},{17,25},{21,29},{10,2},{... | collective-permute-start | bytes 4915208 | tf_op jit(solution)/shard_map/ppermute | solution.py:237
  151.8 43.0 %collective-permute-start.10 = (f32[640,640]{1,0:T(8,128)S(1)}, f32[640,640]{1,0:T(8,128)}, u32[]{:S(2)}, u32[]{:S(2)}) collective-permute-start(f32[640,640]{1,0:T(8,128)S(1)} %copy-done.15), channel_id=1, source_target_pairs={{0,4},{4,0},{8,12},{12,8},{16,20},{20,16},{24,28},{28,24},{1,5},{5... | collective-permute-start | bytes 4915208 | tf_op jit(solution)/shard_map/ppermute | solution.py:237
  153.2 33.1 %collective-permute-start.16 = (f32[640,512]{1,0:T(8,128)}, f32[640,512]{1,0:T(8,128)}, u32[]{:S(2)}, u32[]{:S(2)}) collective-permute-start(f32[640,512]{1,0:T(8,128)} %collective-permute-done.14), channel_id=1, source_target_pairs={{0,2},{1,3},{2,0},{3,1},{4,6},{5,7},{6,4},{7,5},{8,10},{9,11},{10,... | collective-permute-start | bytes 3932168 | tf_op jit(solution)/shard_map/ppermute | solution.py:336
  182.9 44.1 %collective-permute-start.18 = (f32[640,640]{1,0:T(8,128)}, f32[640,640]{1,0:T(8,128)}, u32[]{:S(2)}, u32[]{:S(2)}) collective-permute-start(f32[640,640]{1,0:T(8,128)} %collective-permute-done.13), channel_id=1, source_target_pairs={{8,0},{12,4},{16,24},{20,28},{9,1},{13,5},{17,25},{21,29},{10,2},{... | collective-permute-start | bytes 4915208 | tf_op jit(solution)/shard_map/ppermute | solution.py:237
  184.2 42.8 %collective-permute-start.19 = (f32[640,640]{1,0:T(8,128)}, f32[640,640]{1,0:T(8,128)}, u32[]{:S(2)}, u32[]{:S(2)}) collective-permute-start(f32[640,640]{1,0:T(8,128)} %broadcast_select_fusion.1.refs_4_), channel_id=1, source_target_pairs={{0,4},{4,0},{8,12},{12,8},{16,20},{20,16},{24,28},{28,24},{1,5},{5... | collective-permute-start | bytes 4915208 | tf_op jit(solution)/shard_map/ppermute | solution.py:237
  218.4 42.5 %collective-permute-start.17 = (f32[640,640]{1,0:T(8,128)S(1)}, f32[640,640]{1,0:T(8,128)}, u32[]{:S(2)}, u32[]{:S(2)}) collective-permute-start(f32[640,640]{1,0:T(8,128)S(1)} %broadcast_select_fusion.2.refs_3_), channel_id=1, source_target_pairs={{0,4},{4,0},{8,12},{12,8},{16,20},{20,16},{24,28},{28,24},{1,5},{5... | collective-permute-start | bytes 4915208 | tf_op jit(solution)/shard_map/ppermute | solution.py:237
  250.4 45.5 %collective-permute-start.22 = (f32[640,640]{1,0:T(8,128)S(1)}, f32[640,640]{1,0:T(8,128)}, u32[]{:S(2)}, u32[]{:S(2)}) collective-permute-start(f32[640,640]{1,0:T(8,128)S(1)} %broadcast_select_fusion.refs_3_), channel_id=1, source_target_pairs={{0,4},{4,0},{8,12},{12,8},{16,20},{20,16},{24,28},{28,24},{1,5},{5... | collective-permute-start | bytes 4915208 | tf_op jit(solution)/shard_map/ppermute | solution.py:237
  284.2 38.6 %collective-permute-start.20 = (f32[1280,640]{1,0:T(8,128)}, f32[1280,640]{1,0:T(8,128)}, u32[]{:S(2)}, u32[]{:S(2)}) collective-permute-start(f32[1280,640]{1,0:T(8,128)} %get-tuple-element.93), channel_id=1, source_target_pairs={{0,1},{1,0},{2,3},{3,2},{4,5},{5,4},{6,7},{7,6},{8,9},{9,8},{10,11... | collective-permute-start | bytes 9830408 | tf_op jit(solution)/shard_map/ppermute | solution.py:286
  284.3 35.2 %collective-permute-start.25 = (f32[640,256]{1,0:T(8,128)S(1)}, f32[640,256]{1,0:T(8,128)S(1)}, u32[]{:S(2)}, u32[]{:S(2)}) collective-permute-start(f32[640,256]{1,0:T(8,128)S(1)} %copy-done), channel_id=1, source_target_pairs={{8,16},{12,20},{16,8},{20,12},{9,17},{13,21},{17,9},{21,13},{10,18... | collective-permute-start | bytes 1966088 | tf_op jit(solution)/shard_map/ppermute | solution.py:237
  285.2 34.3 %collective-permute-start.24 = (f32[640,256]{1,0:T(8,128)S(1)}, f32[640,256]{1,0:T(8,128)S(1)}, u32[]{:S(2)}, u32[]{:S(2)}) collective-permute-start(f32[640,256]{1,0:T(8,128)S(1)} %copy-done), channel_id=1, source_target_pairs={{0,8},{4,12},{8,0},{12,4},{16,24},{20,28},{24,16},{28,20},{1,9},{5... | collective-permute-start | bytes 1966088 | tf_op jit(solution)/shard_map/ppermute | solution.py:237
  295.1 24.3 %collective-permute-start.23 = (f32[640,256]{1,0:T(8,128)S(1)}, f32[640,256]{1,0:T(8,128)S(1)}, u32[]{:S(2)}, u32[]{:S(2)}) collective-permute-start(f32[640,256]{1,0:T(8,128)S(1)} %copy-done), channel_id=1, source_target_pairs={{0,4},{4,0},{8,12},{12,8},{16,20},{20,16},{24,28},{28,24},{1,5},{5... | collective-permute-start | bytes 1966088 | tf_op jit(solution)/shard_map/ppermute | solution.py:237
  319.4 27.8 %collective-permute-start.26 = (f32[1280,640]{1,0:T(8,128)}, f32[1280,640]{1,0:T(8,128)}, u32[]{:S(2)}, u32[]{:S(2)}) collective-permute-start(f32[1280,640]{1,0:T(8,128)} %get-tuple-element.101), channel_id=1, source_target_pairs={{0,1},{1,0},{2,3},{3,2},{4,5},{5,4},{6,7},{7,6},{8,9},{9,8},{10,11... | collective-permute-start | bytes 9830408 | tf_op jit(solution)/shard_map/ppermute | solution.py:286
  319.5 19.2 %collective-permute-start.29 = (f32[640,256]{1,0:T(8,128)S(1)}, f32[640,256]{1,0:T(8,128)S(1)}, u32[]{:S(2)}, u32[]{:S(2)}) collective-permute-start(f32[640,256]{1,0:T(8,128)S(1)} %collective-permute-done.24.refs_4_), channel_id=1, source_target_pairs={{0,4},{4,0},{8,12},{12,8},{16,20},{20,16},{24,28},{28,24},{1,5},{5... | collective-permute-start | bytes 1966088 | tf_op jit(solution)/shard_map/ppermute | solution.py:237
  320.9 17.9 %collective-permute-start.28 = (f32[640,256]{1,0:T(8,128)S(1)}, f32[640,256]{1,0:T(8,128)S(1)}, u32[]{:S(2)}, u32[]{:S(2)}) collective-permute-start(f32[640,256]{1,0:T(8,128)S(1)} %collective-permute-done.24.refs_4_), channel_id=1, source_target_pairs={{8,16},{12,20},{16,8},{20,12},{9,17},{13,21},{17,9},{21,13},{10,18... | collective-permute-start | bytes 1966088 | tf_op jit(solution)/shard_map/ppermute | solution.py:237
  321.6 22.6 %collective-permute-start.30 = (f32[640,256]{1,0:T(8,128)S(1)}, f32[640,256]{1,0:T(8,128)S(1)}, u32[]{:S(2)}, u32[]{:S(2)}) collective-permute-start(f32[640,256]{1,0:T(8,128)S(1)} %collective-permute-done.25), channel_id=1, source_target_pairs={{8,0},{12,4},{16,24},{20,28},{9,1},{13,5},{17,25},{21,29},{10,2},{... | collective-permute-start | bytes 1966088 | tf_op jit(solution)/shard_map/ppermute | solution.py:237
  327.4 54.3 %collective-permute-start.21 = (f32[640,640]{1,0:T(8,128)}, f32[640,640]{1,0:T(8,128)}, u32[]{:S(2)}, u32[]{:S(2)}) collective-permute-start(f32[640,640]{1,0:T(8,128)} %slice_bitcast_fusion.2), channel_id=1, source_target_pairs={{0,2},{1,3},{2,0},{3,1},{4,6},{5,7},{6,4},{7,5},{8,10},{9,11},{10,... | collective-permute-start | bytes 4915208 | tf_op jit(solution)/shard_map/ppermute | solution.py:286
  344.2 21.5 %collective-permute-start.31 = (f32[640,256]{1,0:T(8,128)S(1)}, f32[640,256]{1,0:T(8,128)S(1)}, u32[]{:S(2)}, u32[]{:S(2)}) collective-permute-start(f32[640,256]{1,0:T(8,128)S(1)} %collective-permute-done.28), channel_id=1, source_target_pairs={{8,0},{12,4},{16,24},{20,28},{9,1},{13,5},{17,25},{21,29},{10,2},{... | collective-permute-start | bytes 1966088 | tf_op jit(solution)/shard_map/ppermute | solution.py:237
  345.6 20.2 %collective-permute-start.32 = (f32[640,256]{1,0:T(8,128)S(1)}, f32[640,256]{1,0:T(8,128)S(1)}, u32[]{:S(2)}, u32[]{:S(2)}) collective-permute-start(f32[640,256]{1,0:T(8,128)S(1)} %broadcast_select_fusion.4.refs_5_), channel_id=1, source_target_pairs={{0,4},{4,0},{8,12},{12,8},{16,20},{20,16},{24,28},{28,24},{1,5},{5... | collective-permute-start | bytes 1966088 | tf_op jit(solution)/shard_map/ppermute | solution.py:237
  366.3 39.3 %collective-permute-start.27 = (f32[640,640]{1,0:T(8,128)}, f32[640,640]{1,0:T(8,128)}, u32[]{:S(2)}, u32[]{:S(2)}) collective-permute-start(f32[640,640]{1,0:T(8,128)} %slice_bitcast_fusion), channel_id=1, source_target_pairs={{0,2},{1,3},{2,0},{3,1},{4,6},{5,7},{6,4},{7,5},{8,10},{9,11},{10,... | collective-permute-start | bytes 4915208 | tf_op jit(solution)/shard_map/ppermute | solution.py:286
  (55 other events, 611.9 us)

commit v3 on v2

--- a/solution.py
+++ b/solution.py
@@ -363,6 +363,9 @@
             start(k + 1)
             continue
         last = step == 3
+        if k == len(ticks) - 1:
+            first_terms = transposed_product(masked[0], follow(jnp.concatenate(parts[0], axis=1), tokens[-1:]))
+            want(k, first_terms)
         *sums, token = add_products(
             ainv, own_c, [c[0] for c in chosen], [c[1] for c in chosen], group.running, depth,
             parted=last, after=arrived[k] + tokens[-1:] + due.get(k, []),
@@ -395,7 +398,8 @@
             if member == sups - 1 and group is not last_group:
                 last_terms.append(transposed_product(masked[member], follow(part, tokens[-1:])))
     u_whole = [jnp.concatenate(part, axis=1) for part in parts]
-    terms = [transposed_product(masked[m], follow(u_whole[m], others_after)) for m in range(sups - 1)]
+    terms = [transposed_product(masked[m], follow(u_whole[m], others_after)) for m in range(1, sups - 1)]
+    terms = [first_terms] + terms
     other_diag = sum_diagonal(jnp.stack(terms), pcol_bits[:1])
     return jnp.stack(u_whole), dinv - jnp.concatenate([other_diag, last_diag], axis=0)
 

time: 475 us -> 502 us (1.057)
  waiting for transfers between devices: 127 us -> 150 us
    ppermute x3, waiting for transfers between devices: 0.01 us -> 18.4 us  [exchange_near(): lax.ppermute(follow(value, after), 'pcol', pcol_pairs(bit))]
  transfers between devices with their start and end apart: 46 -> 46, of which waited for: 18 -> 18; matrix products, arithmetic and copies ran while one was open for 11% -> 10% of each run, Pallas kernels for 46% -> 44%
where the time goes in v3:
time: 502 us; the launch traced here: 495 us
  Pallas kernels  217 us (43%)
  waiting for transfers between devices  150 us (30%)
  starting transfers between devices  61.1 us (12%)
  other arithmetic  34.9 us (7%)
  local copies, waits for them, and re-layouts  19.6 us (4%)
  matrix products  8.51 us (2%)
    pallas_call x11, Pallas kernels, add_products(): pl.pallas_call(functools.partial(product_kernel, tuple((len(item) for ite...  217 us
    ppermute x27, waiting for transfers between devices, moves(): lax.ppermute(follow(value, after), 'prow', pairs)  103 us
    ppermute x27, starting transfers between devices, moves(): lax.ppermute(follow(value, after), 'prow', pairs)  47.5 us
    ppermute x6, waiting for transfers between devices, sum_diagonal(): value = keep + lax.ppermute(send, 'prow', prow_pairs(bit))  23.1 us
    ppermute x3, waiting for transfers between devices, exchange_near(): lax.ppermute(follow(value, after), 'pcol', pcol_pairs(bit))  18.4 us
  transfers between devices with their start and end apart: 46, of which 18 were waited for; matrix products, arithmetic and copies ran while one was open for 10% of the time, Pallas kernels for 44%

profile of v3, /device:TPU:0, one launch (start us, length us, event | category | flops | bytes accessed | tf_op | source)
XLA Modules:
  0.0 494.7 jit_solution(10250430757638907015)
XLA Ops:
  10.2 3.3 collective-permute-start
  18.6 28.3 %collective-permute-done.1.refs_4_ = f32[640,640]{1,0:T(8,128)} collective-permute-done((f32[640,640]{1,0:T(8,128)S(1)}, f32[640,640]{1,0:T(8,128)}, u32[]{:S(2)}, u32[]{:S(2)}) %collective-permute-start.1) | collective-permute-done | bytes 1638432 | tf_op jit(solution)/shard_map/ppermute | solution.py:237
  46.9 3.4 collective-permute-done.refs_3_
  50.3 20.7 %shard_map.95 = (f32[2560,640]{1,0:T(8,128)}, f32[8,128]{1,0:T(8,128)}) custom-call(s32[3]{0:T(128)S(1)} %pad_add_fusion.1.refs_0_, f32[2560,5120]{1,0:T(8,128)} %refs_3_.3, f32[2560,5120]{1,0:T(8,128)} %refs_3_.3, f32[640,640]{1,0:T(8,128)S(1)} %pad_maximum_fusion.1.refs_3_, f32[640,640]{1,0:T(8,128)} %collective-permute-done.1.refs_4_), custom_call_target="tpu_custom_call" | custom-call | flops 1 | bytes 1 | tf_op jit(solution)/shard_map/pallas_call | solution.py:134
  74.7 9.3 %collective-permute-done.7.refs_3_ = f32[640,640]{1,0:T(8,128)} collective-permute-done((f32[640,640]{1,0:T(8,128)S(1)}, f32[640,640]{1,0:T(8,128)}, u32[]{:S(2)}, u32[]{:S(2)}) %collective-permute-start.7) | collective-permute-done | bytes 1638432 | tf_op jit(solution)/shard_map/ppermute | solution.py:237
  83.9 20.7 %shard_map.96 = (f32[2560,640]{1,0:T(8,128)}, f32[8,128]{1,0:T(8,128)}) custom-call(s32[3]{0:T(128)S(1)} %pad_add_fusion.1.refs_0_, f32[2560,5120]{1,0:T(8,128)} %refs_3_.3, f32[2560,5120]{1,0:T(8,128)} %refs_3_.3, f32[640,640]{1,0:T(8,128)S(1)} %pad_maximum_fusion.2.refs_3_, f32[640,640]{1,0:T(8,128)} %collective-permute-done.6.refs_4_), custom_call_target="tpu_custom_call" | custom-call | flops 1 | bytes 1 | tf_op jit(solution)/shard_map/pallas_call | solution.py:134
  107.0 10.2 %collective-permute-done.4.refs_4_ = f32[640,640]{1,0:T(8,128)} collective-permute-done((f32[640,640]{1,0:T(8,128)}, f32[640,640]{1,0:T(8,128)}, u32[]{:S(2)}, u32[]{:S(2)}) %collective-permute-start.4) | collective-permute-done | bytes 1638432 | tf_op jit(solution)/shard_map/ppermute | solution.py:237
  124.3 23.1 %shard_map.97 = (f32[2560,640]{1,0:T(8,128)}, f32[8,128]{1,0:T(8,128)}) custom-call(s32[3]{0:T(128)S(1)} %pad_add_fusion.2.refs_0_, f32[2560,5120]{1,0:T(8,128)} %refs_3_.3, f32[2560,5120]{1,0:T(8,128)} %refs_3_.3, f32[640,640]{1,0:T(8,128)} %collective-permute-done.refs_3_, ...), custom_call_target="tpu_custom_call", output_to_operand_aliasing={{0}: (5, {})} | custom-call | flops 1 | bytes 1 | tf_op jit(solution)/shard_map/pallas_call | solution.py:134
  153.2 8.1 %collective-permute-done.12 = f32[640,640]{1,0:T(8,128)} collective-permute-done((f32[640,640]{1,0:T(8,128)}, f32[640,640]{1,0:T(8,128)}, u32[]{:S(2)}, u32[]{:S(2)}) %collective-permute-start.12) | collective-permute-done | bytes 1638432 | tf_op jit(solution)/shard_map/ppermute | solution.py:237
  164.1 22.2 %shard_map.98 = (f32[2560,640]{1,0:T(8,128)}, f32[8,128]{1,0:T(8,128)}) custom-call(s32[3]{0:T(128)S(1)} %pad_add_fusion.2.refs_0_, f32[2560,5120]{1,0:T(8,128)} %refs_3_.3, f32[2560,5120]{1,0:T(8,128)} %refs_3_.3, f32[640,640]{1,0:T(8,128)} %collective-permute-done.7.refs_3_, ...), custom_call_target="tpu_custom_call", output_to_operand_aliasing={{0}: (5, {})} | custom-call | flops 1 | bytes 1 | tf_op jit(solution)/shard_map/pallas_call | solution.py:134
  191.4 18.4 %collective-permute-done.16 = f32[640,512]{1,0:T(8,128)} collective-permute-done((f32[640,512]{1,0:T(8,128)}, f32[640,512]{1,0:T(8,128)}, u32[]{:S(2)}, u32[]{:S(2)}) %collective-permute-start.16) | collective-permute-done | bytes 1310752 | tf_op jit(solution)/shard_map/ppermute | solution.py:336
  211.5 21.9 %shard_map.99 = (f32[2560,640]{1,0:T(8,128)}, f32[8,128]{1,0:T(8,128)}) custom-call(s32[3]{0:T(128)S(1)} %pad_add_fusion.3.refs_0_, f32[2560,5120]{1,0:T(8,128)} %refs_3_.3, f32[2560,5120]{1,0:T(8,128)} %refs_3_.3, f32[640,640]{1,0:T(8,128)S(1)} %broadcast_select_fusion.2.refs_3_, ...), custom_call_target="tpu_custom_call", output_to_operand_aliasing={{0}: (5, {})} | custom-call | flops 1 | bytes 1 | tf_op jit(solution)/shard_map/pallas_call | solution.py:134
  235.3 21.7 %shard_map.100 = (f32[2560,640]{1,0:T(8,128)}, f32[8,128]{1,0:T(8,128)}) custom-call(s32[3]{0:T(128)S(1)} %pad_add_fusion.3.refs_0_, f32[2560,5120]{1,0:T(8,128)} %refs_3_.3, f32[2560,5120]{1,0:T(8,128)} %refs_3_.3, f32[640,640]{1,0:T(8,128)S(1)} %broadcast_select_fusion.refs_3_, ...), custom_call_target="tpu_custom_call", output_to_operand_aliasing={{0}: (5, {})} | custom-call | flops 1 | bytes 1 | tf_op jit(solution)/shard_map/pallas_call | solution.py:134
  258.8 13.4 %collective-permute-done.17.refs_3_ = f32[640,640]{1,0:T(8,128)} collective-permute-done((f32[640,640]{1,0:T(8,128)S(1)}, f32[640,640]{1,0:T(8,128)}, u32[]{:S(2)}, u32[]{:S(2)}) %collective-permute-start.17) | collective-permute-done | bytes 1638432 | tf_op jit(solution)/shard_map/ppermute | solution.py:237
  272.2 23.3 %shard_map.101 = (f32[1280,640]{1,0:T(8,128)}, f32[1280,640]{1,0:T(8,128)}, f32[8,128]{1,0:T(8,128)}) custom-call(s32[3]{0:T(128)S(1)} %pad_add_fusion.refs_0_, f32[2560,5120]{1,0:T(8,128)} %refs_3_.3, f32[2560,5120]{1,0:T(8,128)} %refs_3_.3, f32[640,640]{1,0:T(8,128)} %collective-permute-done.17.refs_3_, f32[640,640]{1,0:T(8,128)} %collective-permute-done.10.refs_4_, ...), custom_call_target="tpu_custom_call" | custom-call | flops 1 | bytes 1 | tf_op jit(solution)/shard_map/pallas_call | solution.py:134
  297.2 9.8 %collective-permute-start.24 = (f32[640,256]{1,0:T(8,128)S(1)}, f32[640,256]{1,0:T(8,128)}, u32[]{:S(2)}, u32[]{:S(2)}) collective-permute-start(f32[640,256]{1,0:T(8,128)S(1)} %copy-done), channel_id=1, source_target_pairs={{0,8},{4,12},{8,0},{12,4},{16,24},{20,28},{24,16},{28,20},{1,9},{5... | collective-permute-start | bytes 1966088 | tf_op jit(solution)/shard_map/ppermute | solution.py:237
  307.6 23.6 %shard_map.102 = (f32[1280,640]{1,0:T(8,128)}, f32[1280,640]{1,0:T(8,128)}, f32[8,128]{1,0:T(8,128)}) custom-call(s32[3]{0:T(128)S(1)} %pad_add_fusion.refs_0_, f32[2560,5120]{1,0:T(8,128)} %refs_3_.3, f32[2560,5120]{1,0:T(8,128)} %refs_3_.3, f32[640,640]{1,0:T(8,128)} %collective-permute-done.22.refs_3_, f32[640,640]{1,0:T(8,128)} %collective-permute-done.19.refs_4_, ...), custom_call_target="tpu_custom_call" | custom-call | flops 1 | bytes 1 | tf_op jit(solution)/shard_map/pallas_call | solution.py:134
  338.8 10.3 %shard_map.103 = (f32[2560,256]{1,0:T(8,128)}, f32[8,128]{1,0:T(8,128)}) custom-call(s32[3]{0:T(128)S(1)} %copy-done.2, f32[2560,5120]{1,0:T(8,128)} %refs_3_.3, f32[2560,5120]{1,0:T(8,128)} %refs_3_.3, f32[640,256]{1,0:T(8,128)S(1)} %copy-done, f32[640,256]{1,0:T(8,128)S(1)} %collective-permute-done.23.refs_4_), custom_call_target="tpu_custom_call" | custom-call | flops 1 | bytes 1 | tf_op jit(solution)/shard_map/pallas_call | solution.py:134
  349.1 3.4 collective-permute-done.29.refs_6_
  352.5 10.5 %collective-permute-done.30 = f32[640,256]{1,0:T(8,128)} collective-permute-done((f32[640,256]{1,0:T(8,128)}, f32[640,256]{1,0:T(8,128)}, u32[]{:S(2)}, u32[]{:S(2)}) %collective-permute-start.30) | collective-permute-done | bytes 655392 | tf_op jit(solution)/shard_map/ppermute | solution.py:237
  367.2 3.3 add.179
  373.3 7.2 %collective-permute-done.31 = f32[640,256]{1,0:T(8,128)S(1)} collective-permute-done((f32[640,256]{1,0:T(8,128)S(1)}, f32[640,256]{1,0:T(8,128)S(1)}, u32[]{:S(2)}, u32[]{:S(2)}) %collective-permute-start.31) | collective-permute-done | bytes 655392 | tf_op jit(solution)/shard_map/ppermute | solution.py:237
  380.7 14.9 %shard_map.104 = (f32[2560,256]{1,0:T(8,128)}, f32[8,128]{1,0:T(8,128)}) custom-call(s32[4]{0:T(128)S(1)} %pad_add_fusion.5.refs_0_, f32[2560,5120]{1,0:T(8,128)} %refs_3_.3, f32[2560,5120]{1,0:T(8,128)} %refs_3_.3, f32[2560,5120]{1,0:T(8,128)} %refs_3_.3, f32[640,256]{1,0:T(8,128)} %collective-permute-done.24.refs_4_, ...), custom_call_target="tpu_custom_call", output_to_operand_aliasing={{0}: (7, {})} | custom-call | flops 1 | bytes 1 | tf_op jit(solution)/shard_map/pallas_call | solution.py:134
  401.4 9.0 %collective-permute-done.33.refs_6_ = f32[640,256]{1,0:T(8,128)S(1)} collective-permute-done((f32[640,256]{1,0:T(8,128)S(1)}, f32[640,256]{1,0:T(8,128)S(1)}, u32[]{:S(2)}, u32[]{:S(2)}) %collective-permute-start.33) | collective-permute-done | bytes 655392 | tf_op jit(solution)/shard_map/ppermute | solution.py:237
  410.4 14.5 %shard_map.105 = (f32[1280,256]{1,0:T(8,128)}, f32[1280,256]{1,0:T(8,128)}, f32[8,128]{1,0:T(8,128)}) custom-call(s32[4]{0:T(128)S(1)} %pad_add_fusion.4.refs_0_, f32[2560,5120]{1,0:T(8,128)} %refs_3_.3, f32[2560,5120]{1,0:T(8,128)} %refs_3_.3, f32[2560,5120]{1,0:T(8,128)} %refs_3_.3, f32[640,256]{1,0:T(8,128)S(1)} %broadcast_select_fusion.5.refs_4_, ...), custom_call_target="tpu_custom_call" | custom-call | flops 1 | bytes 1 | tf_op jit(solution)/shard_map/pallas_call | solution.py:134
  425.0 3.5 fusion.4
  452.8 5.4 %collective-permute-done.43 = f32[2,2,64,128]{3,2,1,0:T(8,128)S(1)} collective-permute-done((f32[2,2,64,128]{3,2,1,0:T(8,128)}, f32[2,2,64,128]{3,2,1,0:T(8,128)S(1)}, u32[]{:S(2)}, u32[]{:S(2)}) %collective-permute-start.43) | collective-permute-done | bytes 131104 | tf_op jit(solution)/shard_map/ppermute | solution.py:316
  462.0 3.2 collective-permute-done.44
  466.1 4.1 collective-permute-done.45
  470.2 4.5 collective-permute-done.39
  476.6 5.2 %collective-permute-done.40 = f32[4,2,64,128]{3,2,1,0:T(8,128)S(1)} collective-permute-done((f32[4,2,64,128]{3,2,1,0:T(8,128)S(1)}, f32[4,2,64,128]{3,2,1,0:T(8,128)S(1)}, u32[]{:S(2)}, u32[]{:S(2)}) %collective-permute-start.40) | collective-permute-done | bytes 262176 | tf_op jit(solution)/shard_map/ppermute | solution.py:316
  484.3 4.9 collective-permute-done.41
  (218 shorter events, 105.7 us)
Async XLA Ops:
  7.2 39.7 %collective-permute-start.1 = (f32[640,640]{1,0:T(8,128)S(1)}, f32[640,640]{1,0:T(8,128)}, u32[]{:S(2)}, u32[]{:S(2)}) collective-permute-start(f32[640,640]{1,0:T(8,128)S(1)} %pad_maximum_fusion.1.refs_3_), channel_id=1, source_target_pairs={{0,4},{4,0},{8,12},{12,8},{16,20},{20,16},{24,28},{28,24},{1,5},{5... | collective-permute-start | bytes 4915208 | tf_op jit(solution)/shard_map/ppermute | solution.py:237
  10.2 40.1 %collective-permute-start = (f32[640,640]{1,0:T(8,128)S(1)}, f32[640,640]{1,0:T(8,128)}, u32[]{:S(2)}, u32[]{:S(2)}) collective-permute-start(f32[640,640]{1,0:T(8,128)S(1)} %pad_maximum_fusion.1.refs_3_), channel_id=1, source_target_pairs={{0,8},{4,12},{8,0},{12,4},{16,24},{20,28},{24,16},{28,20},{1,9},{5... | collective-permute-start | bytes 4915208 | tf_op jit(solution)/shard_map/ppermute | solution.py:237
  14.6 58.8 %collective-permute-start.8 = (f32[640,640]{1,0:T(8,128)S(1)}, f32[640,640]{1,0:T(8,128)}, u32[]{:S(2)}, u32[]{:S(2)}) collective-permute-start(f32[640,640]{1,0:T(8,128)S(1)} %pad_maximum_fusion.2.refs_3_), channel_id=1, source_target_pairs={{8,16},{12,20},{16,8},{20,12},{9,17},{13,21},{17,9},{21,13},{10,18... | collective-permute-start | bytes 4915208 | tf_op jit(solution)/shard_map/ppermute | solution.py:237
  16.5 67.4 %collective-permute-start.7 = (f32[640,640]{1,0:T(8,128)S(1)}, f32[640,640]{1,0:T(8,128)}, u32[]{:S(2)}, u32[]{:S(2)}) collective-permute-start(f32[640,640]{1,0:T(8,128)S(1)} %pad_maximum_fusion.2.refs_3_), channel_id=1, source_target_pairs={{0,8},{4,12},{8,0},{12,4},{16,24},{20,28},{24,16},{28,20},{1,9},{5... | collective-permute-start | bytes 4915208 | tf_op jit(solution)/shard_map/ppermute | solution.py:237
  18.1 65.9 %collective-permute-start.6 = (f32[640,640]{1,0:T(8,128)S(1)}, f32[640,640]{1,0:T(8,128)}, u32[]{:S(2)}, u32[]{:S(2)}) collective-permute-start(f32[640,640]{1,0:T(8,128)S(1)} %pad_maximum_fusion.2.refs_3_), channel_id=1, source_target_pairs={{0,4},{4,0},{8,12},{12,8},{16,20},{20,16},{24,28},{28,24},{1,5},{5... | collective-permute-start | bytes 4915208 | tf_op jit(solution)/shard_map/ppermute | solution.py:237
  71.0 46.2 %collective-permute-start.4 = (f32[640,640]{1,0:T(8,128)}, f32[640,640]{1,0:T(8,128)}, u32[]{:S(2)}, u32[]{:S(2)}) collective-permute-start(f32[640,640]{1,0:T(8,128)} %collective-permute-done.refs_3_), channel_id=1, source_target_pairs={{0,4},{4,0},{8,12},{12,8},{16,20},{20,16},{24,28},{28,24},{1,5},{5... | collective-permute-start | bytes 4915208 | tf_op jit(solution)/shard_map/ppermute | solution.py:237
  71.6 45.6 %collective-permute-start.3 = (f32[640,640]{1,0:T(8,128)}, f32[640,640]{1,0:T(8,128)}, u32[]{:S(2)}, u32[]{:S(2)}) collective-permute-start(f32[640,640]{1,0:T(8,128)} %collective-permute-done.refs_3_), channel_id=1, source_target_pairs={{8,16},{12,20},{16,8},{20,12},{9,17},{13,21},{17,9},{21,13},{10,18... | collective-permute-start | bytes 4915208 | tf_op jit(solution)/shard_map/ppermute | solution.py:237
  73.4 48.2 %collective-permute-start.5 = (f32[640,640]{1,0:T(8,128)}, f32[640,640]{1,0:T(8,128)}, u32[]{:S(2)}, u32[]{:S(2)}) collective-permute-start(f32[640,640]{1,0:T(8,128)} %collective-permute-done.2), channel_id=1, source_target_pairs={{8,0},{12,4},{16,24},{20,28},{9,1},{13,5},{17,25},{21,29},{10,2},{... | collective-permute-start | bytes 4915208 | tf_op jit(solution)/shard_map/ppermute | solution.py:237
  104.6 46.1 %collective-permute-start.13 = (f32[640,640]{1,0:T(8,128)}, f32[640,640]{1,0:T(8,128)}, u32[]{:S(2)}, u32[]{:S(2)}) collective-permute-start(f32[640,640]{1,0:T(8,128)} %collective-permute-done.7.refs_3_), channel_id=1, source_target_pairs={{8,16},{12,20},{16,8},{20,12},{9,17},{13,21},{17,9},{21,13},{10,18... | collective-permute-start | bytes 4915208 | tf_op jit(solution)/shard_map/ppermute | solution.py:237
  106.5 45.9 %collective-permute-start.11 = (f32[640,640]{1,0:T(8,128)}, f32[640,640]{1,0:T(8,128)}, u32[]{:S(2)}, u32[]{:S(2)}) collective-permute-start(f32[640,640]{1,0:T(8,128)} %collective-permute-done.7.refs_3_), channel_id=1, source_target_pairs={{0,4},{4,0},{8,12},{12,8},{16,20},{20,16},{24,28},{28,24},{1,5},{5... | collective-permute-start | bytes 4915208 | tf_op jit(solution)/shard_map/ppermute | solution.py:237
  117.2 31.6 %collective-permute-start.14 = (f32[640,512]{1,0:T(8,128)S(1)}, f32[640,512]{1,0:T(8,128)}, u32[]{:S(2)}, u32[]{:S(2)}) collective-permute-start(f32[640,512]{1,0:T(8,128)S(1)} %copy-done.4), channel_id=1, source_target_pairs={{0,1},{1,0},{2,3},{3,2},{4,5},{5,4},{6,7},{7,6},{8,9},{9,8},{10,11... | collective-permute-start | bytes 3932168 | tf_op jit(solution)/shard_map/ppermute | solution.py:336
  117.2 44.1 %collective-permute-start.12 = (f32[640,640]{1,0:T(8,128)}, f32[640,640]{1,0:T(8,128)}, u32[]{:S(2)}, u32[]{:S(2)}) collective-permute-start(f32[640,640]{1,0:T(8,128)} %collective-permute-done.8), channel_id=1, source_target_pairs={{8,0},{12,4},{16,24},{20,28},{9,1},{13,5},{17,25},{21,29},{10,2},{... | collective-permute-start | bytes 4915208 | tf_op jit(solution)/shard_map/ppermute | solution.py:237
  147.4 62.4 %collective-permute-start.9 = (f32[640,640]{1,0:T(8,128)}, f32[640,640]{1,0:T(8,128)}, u32[]{:S(2)}, u32[]{:S(2)}) collective-permute-start(f32[640,640]{1,0:T(8,128)} %collective-permute-done.3), channel_id=1, source_target_pairs={{8,0},{12,4},{16,24},{20,28},{9,1},{13,5},{17,25},{21,29},{10,2},{... | collective-permute-start | bytes 4915208 | tf_op jit(solution)/shard_map/ppermute | solution.py:237
  148.8 61.1 %collective-permute-start.10 = (f32[640,640]{1,0:T(8,128)S(1)}, f32[640,640]{1,0:T(8,128)}, u32[]{:S(2)}, u32[]{:S(2)}) collective-permute-start(f32[640,640]{1,0:T(8,128)S(1)} %copy-done.15), channel_id=1, source_target_pairs={{0,4},{4,0},{8,12},{12,8},{16,20},{20,16},{24,28},{28,24},{1,5},{5... | collective-permute-start | bytes 4915208 | tf_op jit(solution)/shard_map/ppermute | solution.py:237
  150.7 36.8 %collective-permute-start.15 = (f32[640,512]{1,0:T(8,128)S(1)}, f32[640,512]{1,0:T(8,128)S(1)}, u32[]{:S(2)}, u32[]{:S(2)}) collective-permute-start(f32[640,512]{1,0:T(8,128)S(1)} %copy-done.4), channel_id=1, source_target_pairs={{0,2},{1,3},{2,0},{3,1},{4,6},{5,7},{6,4},{7,5},{8,10},{9,11},{10,... | collective-permute-start | bytes 3932168 | tf_op jit(solution)/shard_map/ppermute | solution.py:336
  152.4 57.5 %collective-permute-start.16 = (f32[640,512]{1,0:T(8,128)}, f32[640,512]{1,0:T(8,128)}, u32[]{:S(2)}, u32[]{:S(2)}) collective-permute-start(f32[640,512]{1,0:T(8,128)} %collective-permute-done.14), channel_id=1, source_target_pairs={{0,2},{1,3},{2,0},{3,1},{4,6},{5,7},{6,4},{7,5},{8,10},{9,11},{10,... | collective-permute-start | bytes 3932168 | tf_op jit(solution)/shard_map/ppermute | solution.py:336
  186.2 47.5 %collective-permute-start.18 = (f32[640,640]{1,0:T(8,128)}, f32[640,640]{1,0:T(8,128)}, u32[]{:S(2)}, u32[]{:S(2)}) collective-permute-start(f32[640,640]{1,0:T(8,128)} %collective-permute-done.13), channel_id=1, source_target_pairs={{8,0},{12,4},{16,24},{20,28},{9,1},{13,5},{17,25},{21,29},{10,2},{... | collective-permute-start | bytes 4915208 | tf_op jit(solution)/shard_map/ppermute | solution.py:237
  188.6 45.2 %collective-permute-start.19 = (f32[640,640]{1,0:T(8,128)}, f32[640,640]{1,0:T(8,128)}, u32[]{:S(2)}, u32[]{:S(2)}) collective-permute-start(f32[640,640]{1,0:T(8,128)} %broadcast_select_fusion.1.refs_4_), channel_id=1, source_target_pairs={{0,4},{4,0},{8,12},{12,8},{16,20},{20,16},{24,28},{28,24},{1,5},{5... | collective-permute-start | bytes 4915208 | tf_op jit(solution)/shard_map/ppermute | solution.py:237
  233.4 38.8 %collective-permute-start.17 = (f32[640,640]{1,0:T(8,128)S(1)}, f32[640,640]{1,0:T(8,128)}, u32[]{:S(2)}, u32[]{:S(2)}) collective-permute-start(f32[640,640]{1,0:T(8,128)S(1)} %broadcast_select_fusion.2.refs_3_), channel_id=1, source_target_pairs={{0,4},{4,0},{8,12},{12,8},{16,20},{20,16},{24,28},{28,24},{1,5},{5... | collective-permute-start | bytes 4915208 | tf_op jit(solution)/shard_map/ppermute | solution.py:237
  257.1 50.6 %collective-permute-start.22 = (f32[640,640]{1,0:T(8,128)S(1)}, f32[640,640]{1,0:T(8,128)}, u32[]{:S(2)}, u32[]{:S(2)}) collective-permute-start(f32[640,640]{1,0:T(8,128)S(1)} %broadcast_select_fusion.refs_3_), channel_id=1, source_target_pairs={{0,4},{4,0},{8,12},{12,8},{16,20},{20,16},{24,28},{28,24},{1,5},{5... | collective-permute-start | bytes 4915208 | tf_op jit(solution)/shard_map/ppermute | solution.py:237
  295.5 35.8 %collective-permute-start.20 = (f32[1280,640]{1,0:T(8,128)}, f32[1280,640]{1,0:T(8,128)S(1)}, u32[]{:S(2)}, u32[]{:S(2)}) collective-permute-start(f32[1280,640]{1,0:T(8,128)} %get-tuple-element.93), channel_id=1, source_target_pairs={{0,1},{1,0},{2,3},{3,2},{4,5},{5,4},{6,7},{7,6},{8,9},{9,8},{10,11... | collective-permute-start | bytes 9830408 | tf_op jit(solution)/shard_map/ppermute | solution.py:286
  295.5 35.7 %collective-permute-start.25 = (f32[640,256]{1,0:T(8,128)S(1)}, f32[640,256]{1,0:T(8,128)}, u32[]{:S(2)}, u32[]{:S(2)}) collective-permute-start(f32[640,256]{1,0:T(8,128)S(1)} %copy-done), channel_id=1, source_target_pairs={{8,16},{12,20},{16,8},{20,12},{9,17},{13,21},{17,9},{21,13},{10,18... | collective-permute-start | bytes 1966088 | tf_op jit(solution)/shard_map/ppermute | solution.py:237
  297.2 34.0 %collective-permute-start.24 = (f32[640,256]{1,0:T(8,128)S(1)}, f32[640,256]{1,0:T(8,128)}, u32[]{:S(2)}, u32[]{:S(2)}) collective-permute-start(f32[640,256]{1,0:T(8,128)S(1)} %copy-done), channel_id=1, source_target_pairs={{0,8},{4,12},{8,0},{12,4},{16,24},{20,28},{24,16},{28,20},{1,9},{5... | collective-permute-start | bytes 1966088 | tf_op jit(solution)/shard_map/ppermute | solution.py:237
  307.1 24.1 %collective-permute-start.23 = (f32[640,256]{1,0:T(8,128)S(1)}, f32[640,256]{1,0:T(8,128)S(1)}, u32[]{:S(2)}, u32[]{:S(2)}) collective-permute-start(f32[640,256]{1,0:T(8,128)S(1)} %copy-done), channel_id=1, source_target_pairs={{0,4},{4,0},{8,12},{12,8},{16,20},{20,16},{24,28},{28,24},{1,5},{5... | collective-permute-start | bytes 1966088 | tf_op jit(solution)/shard_map/ppermute | solution.py:237
  331.2 36.0 %collective-permute-start.26 = (f32[1280,640]{1,0:T(8,128)}, f32[1280,640]{1,0:T(8,128)}, u32[]{:S(2)}, u32[]{:S(2)}) collective-permute-start(f32[1280,640]{1,0:T(8,128)} %get-tuple-element.101), channel_id=1, source_target_pairs={{0,1},{1,0},{2,3},{3,2},{4,5},{5,4},{6,7},{7,6},{8,9},{9,8},{10,11... | collective-permute-start | bytes 9830408 | tf_op jit(solution)/shard_map/ppermute | solution.py:286
  333.9 63.1 %collective-permute-start.21 = (f32[640,640]{1,0:T(8,128)}, f32[640,640]{1,0:T(8,128)}, u32[]{:S(2)}, u32[]{:S(2)}) collective-permute-start(f32[640,640]{1,0:T(8,128)} %slice_bitcast_fusion.2), channel_id=1, source_target_pairs={{0,2},{1,3},{2,0},{3,1},{4,6},{5,7},{6,4},{7,5},{8,10},{9,11},{10,... | collective-permute-start | bytes 4915208 | tf_op jit(solution)/shard_map/ppermute | solution.py:286
  337.4 25.6 %collective-permute-start.30 = (f32[640,256]{1,0:T(8,128)}, f32[640,256]{1,0:T(8,128)}, u32[]{:S(2)}, u32[]{:S(2)}) collective-permute-start(f32[640,256]{1,0:T(8,128)} %collective-permute-done.25), channel_id=1, source_target_pairs={{8,0},{12,4},{16,24},{20,28},{9,1},{13,5},{17,25},{21,29},{10,2},{... | collective-permute-start | bytes 1966088 | tf_op jit(solution)/shard_map/ppermute | solution.py:237
  363.0 17.6 %collective-permute-start.31 = (f32[640,256]{1,0:T(8,128)S(1)}, f32[640,256]{1,0:T(8,128)S(1)}, u32[]{:S(2)}, u32[]{:S(2)}) collective-permute-start(f32[640,256]{1,0:T(8,128)S(1)} %collective-permute-done.28), channel_id=1, source_target_pairs={{8,0},{12,4},{16,24},{20,28},{9,1},{13,5},{17,25},{21,29},{10,2},{... | collective-permute-start | bytes 1966088 | tf_op jit(solution)/shard_map/ppermute | solution.py:237
  365.7 29.8 %collective-permute-start.32 = (f32[640,256]{1,0:T(8,128)S(1)}, f32[640,256]{1,0:T(8,128)S(1)}, u32[]{:S(2)}, u32[]{:S(2)}) collective-permute-start(f32[640,256]{1,0:T(8,128)S(1)} %broadcast_select_fusion.4.refs_5_), channel_id=1, source_target_pairs={{0,4},{4,0},{8,12},{12,8},{16,20},{20,16},{24,28},{28,24},{1,5},{5... | collective-permute-start | bytes 1966088 | tf_op jit(solution)/shard_map/ppermute | solution.py:237
  372.7 57.2 %collective-permute-start.27 = (f32[640,640]{1,0:T(8,128)}, f32[640,640]{1,0:T(8,128)S(1)}, u32[]{:S(2)}, u32[]{:S(2)}) collective-permute-start(f32[640,640]{1,0:T(8,128)} %slice_bitcast_fusion), channel_id=1, source_target_pairs={{0,2},{1,3},{2,0},{3,1},{4,6},{5,7},{6,4},{7,5},{8,10},{9,11},{10,... | collective-permute-start | bytes 4915208 | tf_op jit(solution)/shard_map/ppermute | solution.py:286
  424.9 17.1 %collective-permute-start.34 = (f32[1280,256]{1,0:T(8,128)}, f32[1280,256]{1,0:T(8,128)}, u32[]{:S(2)}, u32[]{:S(2)}) collective-permute-start(f32[1280,256]{1,0:T(8,128)} %get-tuple-element.117), channel_id=1, source_target_pairs={{0,1},{1,0},{2,3},{3,2},{4,5},{5,4},{6,7},{7,6},{8,9},{9,8},{10,11... | collective-permute-start | bytes 3932168 | tf_op jit(solution)/shard_map/ppermute | solution.py:286
  452.2 18.0 %collective-permute-start.35 = (f32[640,256]{1,0:T(8,128)}, f32[640,256]{1,0:T(8,128)S(1)}, u32[]{:S(2)}, u32[]{:S(2)}) collective-permute-start(f32[640,256]{1,0:T(8,128)} %slice_bitcast_fusion.4), channel_id=1, source_target_pairs={{0,2},{1,3},{2,0},{3,1},{4,6},{5,7},{6,4},{7,5},{8,10},{9,11},{10,... | collective-permute-start | bytes 1966088 | tf_op jit(solution)/shard_map/ppermute | solution.py:286
  (49 other events, 544.2 us)
